TPU v7x, 32 devices: a whole 2x2x4 slice. The times are simulated.
32 devices in a mesh: vol: 4 (over y, core), zs: 8 (over z, x).
Axes of the slice: x: 2, y: 2, z: 4, core: 2. Of those that a mesh axis runs over, the one named last changes fastest.
Arguments:
- volume: bfloat16 [8, 128, 256], P('zs', 'vol'), may hold values from -6 to 6
- first_weight: bfloat16 [9, 12], replicated, may hold values from -3 to 3
- first_offset: float32 [12], replicated, may hold values from -2 to 2
- second_weight: bfloat16 [9, 12, 12], replicated, may hold values from -0.875 to 0.875
- second_offset: float32 [12], replicated, may hold values from -2 to 2
- reduce_conv_weight: bfloat16 [4, 12, 24], replicated, may hold values from -1.25 to 1.25
- reduce_conv_bias: float32 [24], replicated, may hold values from -2 to 2
- deep_weight: bfloat16 [27, 24, 24], replicated, may hold values from -0.3125 to 0.3125
- deep_offset: float32 [24], replicated, may hold values from -2 to 2
Outputs:
- affinity: bfloat16 [8, 24, 64, 128], P(None, None, ('vol', 'zs'))
All inputs are finite; a program needn't handle non-finite values.
Results may differ from a plain program's by a relative error of at most 0.0065.
Values may be sent and summed in bfloat16 or wider, within the bound.
No kernel may reach another device: no remote copies, remote signals or barrier semaphores. Data moves between devices by JAX's collectives and lax.ppermute only.
A program may use at most 192 MiB of HBM per device.

v0:
```python
import jax
import jax.numpy as jnp
from jax import lax
from jax.sharding import PartitionSpec as P


def extended(value, sides, width):
    for axis, dim in sides:
        size, length = (lax.axis_size(axis), value.shape[dim])
        up = [(i, (i + 1) % size) for i in range(size - 1)]
        down = [(j, i) for i, j in up]
        last = lax.slice_in_dim(value, length - width, length, axis=dim)
        first = lax.slice_in_dim(value, 0, width, axis=dim)
        before = lax.ppermute(last, axis, up)
        after = lax.ppermute(first, axis, down)
        value = jnp.concatenate([before, value, after], axis=dim)
    return value


def plane_conv(field, weight, offset):
    padded = jnp.pad(field, ((0, 0), (0, 0), (0, 0), (1, 1)))
    row_count = field.shape[2] - 2
    col_count = field.shape[3]
    summed = jnp.zeros((field.shape[0], weight.shape[2], row_count, col_count), jnp.float32)
    for along_x in range(3):
        for along_y in range(3):
            window = padded[:, :, along_x : along_x + row_count, along_y : along_y + col_count]
            summed = summed + jnp.einsum(
                "zcxy,cd->zdxy",
                window,
                weight[3 * along_x + along_y],
                preferred_element_type=jnp.float32,
            )
    return summed + offset[None, :, None, None]


def leading_section(
    rimmed, at_top, at_bottom, first_weight, first_offset, second_weight, second_offset, rim_rows
):
    field = rimmed[:, None]
    first = jax.nn.relu(plane_conv(field, first_weight[:, None, :], first_offset))
    row_ids = lax.broadcasted_iota(jnp.int32, first.shape, 2)
    last_row = first.shape[2] - 1
    outside = (row_ids < rim_rows - 1) & at_top | (row_ids > last_row - (rim_rows - 1)) & at_bottom
    first = jnp.where(outside, 0.0, first).astype(jnp.bfloat16)
    return jax.nn.relu(plane_conv(first, second_weight, second_offset)).astype(jnp.bfloat16)


def halve_resolution(latter_conv, reduce_conv_weight, reduce_conv_bias):
    depth, channels, fine_rows, fine_cols = latter_conv.shape
    blocks = latter_conv.reshape(depth, channels, fine_rows // 2, 2, fine_cols // 2, 2)
    kernel = reduce_conv_weight.reshape(2, 2, channels, reduce_conv_weight.shape[2])
    summed = jnp.einsum("zcxayb,abcd->zdxy", blocks, kernel, preferred_element_type=jnp.float32)
    return jax.nn.relu(summed + reduce_conv_bias[None, :, None, None]).astype(jnp.bfloat16)


def reduced_row_span(coarse):
    return extended(coarse, ((("vol", "zs"), 2),), 1)


def deep_conv(rimmed, deep_weight, deep_offset):
    padded = jnp.pad(rimmed, ((1, 1), (0, 0), (0, 0), (1, 1)))
    depth = rimmed.shape[0]
    row_count = rimmed.shape[2] - 2
    col_count = rimmed.shape[3]
    summed = jnp.zeros((depth, deep_weight.shape[2], row_count, col_count), jnp.float32)
    for along_z in range(3):
        for along_x in range(3):
            for along_y in range(3):
                window = padded[
                    along_z : along_z + depth,
                    :,
                    along_x : along_x + row_count,
                    along_y : along_y + col_count,
                ]
                summed = summed + jnp.einsum(
                    "zcxy,cd->zdxy",
                    window,
                    deep_weight[9 * along_z + 3 * along_x + along_y],
                    preferred_element_type=jnp.float32,
                )
    return jax.nn.relu(summed + deep_offset[None, :, None, None]).astype(jnp.bfloat16)


def shards(
    volume,
    first_weight,
    first_offset,
    second_weight,
    second_offset,
    reduce_conv_weight,
    reduce_conv_bias,
    deep_weight,
    deep_offset,
):
    rimmed = extended(volume, (("vol", 1),), 2)
    position = lax.axis_index("vol")
    members = lax.axis_size("vol")
    latter_conv = leading_section(
        rimmed,
        position == 0,
        position == members - 1,
        first_weight,
        first_offset,
        second_weight,
        second_offset,
        2,
    )
    resident_reduced = halve_resolution(latter_conv, reduce_conv_weight, reduce_conv_bias)
    coarse = lax.all_to_all(resident_reduced, "zs", split_axis=2, concat_axis=0, tiled=True)
    return deep_conv(reduced_row_span(coarse), deep_weight, deep_offset)


def solution(mesh):
    return jax.shard_map(
        shards,
        mesh=mesh,
        in_specs=(P("zs", "vol", None), P(), P(), P(), P(), P(), P(), P(), P()),
        out_specs=P(None, None, ("vol", "zs"), None),
        check_vma=False,
    )
```

profile of v0, /device:TPU:1, one launch (start us, length us, event | category | flops | bytes accessed | tf_op | source)
XLA Modules:
  0.0 59.4 jit_solution(4523245048099126285)
XLA Ops:
  0.0 0.7 %fusion.163 = (bf16[1,2,256]{2,1,0:T(2,128)(2,1)S(1)}, bf16[1,2,256]{2,1,0:T(2,128)(2,1)S(1)}) fusion(bf16[1,32,256]{2,1,0:T(8,128)(2,1)} %param.9), kind=kLoop, calls=%fused_computation.215 | loop fusion | bytes 4096 | tf_op jit(solution)/shard_map/slice | solution.py:12
  0.7 4.5 %collective-permute-start = (bf16[1,2,256]{2,1,0:T(2,128)(2,1)S(1)}, bf16[1,2,256]{2,1,0:T(2,128)(2,1)S(1)}, u32[]{:S(2)}, u32[]{:S(2)}) collective-permute-start(bf16[1,2,256]{2,1,0:T(2,128)(2,1)S(1)} %get-tuple-element.43), channel_id=1, source_target_pairs={{0,8},{8,16},{16,24},{1,9},{9,17},{17,25},{2,10},{10,18},{18,26},{... | collective-permute-start | bytes 3080 | tf_op jit(solution)/shard_map/ppermute | solution.py:14
  5.3 1.9 %collective-permute-start.1 = (bf16[1,2,256]{2,1,0:T(2,128)(2,1)S(1)}, bf16[1,2,256]{2,1,0:T(2,128)(2,1)S(1)}, u32[]{:S(2)}, u32[]{:S(2)}) collective-permute-start(bf16[1,2,256]{2,1,0:T(2,128)(2,1)S(1)} %get-tuple-element.44), channel_id=1, source_target_pairs={{8,0},{16,8},{24,16},{9,1},{17,9},{25,17},{10,2},{18,10},{26,18},{... | collective-permute-start | bytes 3080 | tf_op jit(solution)/shard_map/ppermute | solution.py:15
  7.2 1.0 %bitcast_convert_fusion.8 = (f32[12]{0:T(128)S(1)}, f32[12]{0:T(128)S(1)}, f32[12]{0:T(128)S(1)}, f32[12]{0:T(128)S(1)}, f32[12]{0:T(128)S(1)}, /*index=5*/f32[1...) fusion(bf16[9,12]{1,0:T(8,128)(2,1)} %param.10), kind=kLoop, calls=%fused_computation.203 | loop fusion | flops 108 | bytes 648 | tf_op jit(solution)/shard_map/convert.37
  8.2 1.9 %collective-permute-done.1 = bf16[1,2,256]{2,1,0:T(2,128)(2,1)S(1)} collective-permute-done((bf16[1,2,256]{2,1,0:T(2,128)(2,1)S(1)}, bf16[1,2,256]{2,1,0:T(2,128)(2,1)S(1)}, u32[]{:S(2)}, u32[]{:S(2)}) %collective-permute-start.1) | collective-permute-done | bytes 1056 | tf_op jit(solution)/shard_map/ppermute | solution.py:15
  10.1 0.7 %maximum_bitcast_fusion = bf16[1,1,36,256]{3,2,1,0:T(8,128)(2,1)S(1)} fusion(bf16[1,2,256]{2,1,0:T(2,128)(2,1)S(1)} %collective-permute-done.1, bf16[1,32,256]{2,1,0:T(8,128)(2,1)} %param.9, bf16[1,2,256]{2,1,0:T(2,128)(2,1)S(1)} %collective-permute-done), kind=kLoop, calls=%fused_computation.146 | loop fusion | flops 55296 | bytes 36864 | tf_op jit(solution)/shard_map/broadcast_in_dim | solution.py:40
  11.0 1.1 %fusion.43 = bf16[1,12,34,256]{3,1,2,0:T(8,128)(2,1)S(1)} fusion(f32[12]{0:T(128)} %param.11, f32[12]{0:T(128)S(1)} %get-tuple-element.52, f32[34,256]{1,0:T(8,128)S(1)} %get-tuple-element.39, f32[12]{0:T(128)S(1)} %get-tuple-element.53, f32[34,256]{1,0:T(8,128)S(1)} %get-tuple-element.40, f32[12]{0:T(128)S(1)} %get-tuple-element.46, ...), kind=kLoop, calls=%fused_computation.78 | loop fusion | flops 2193408 | bytes 522754 | tf_op jit(solution)/shard_map/convert_element_type | solution.py:45
  12.1 1.0 %fusion.45 = f32[32,256,12]{1,2,0:T(8,128)S(1)} fusion(bf16[1,12,34,256]{3,1,2,0:T(8,128)(2,1)S(1)} %fusion.43, bf16[9,12,12]{2,1,0:T(8,128)(2,1)} %param.12), kind=kOutput, calls=%fused_computation.80 | convolution fusion | flops 2359296 | bytes 606208 | tf_op jit(solution)/shard_map/zcxy,cd->zdxy/dot_general | solution.py:28
  13.1 1.0 %convolution_add_fusion.7 = f32[32,256,12]{1,2,0:T(8,128)S(1)} fusion(f32[32,256,12]{1,2,0:T(8,128)S(1)} %fusion.45, bf16[1,12,34,256]{3,1,2,0:T(8,128)(2,1)S(1)} %fusion.43, bf16[9,12,12]{2,1,0:T(8,128)(2,1)} %param.12), kind=kOutput, calls=%fused_computation.13 | convolution fusion | flops 2457600 | bytes 1183744 | tf_op jit(solution)/shard_map/zcxy,cd->zdxy/dot_general | solution.py:28
  14.1 0.3 convolution_add_fusion.6
  14.4 0.3 convolution_add_fusion.5
  14.7 0.3 convolution_add_fusion.4
  15.0 0.3 convolution_add_fusion.3
  15.3 0.3 convolution_add_fusion.2
  15.6 0.3 convolution_add_fusion.1
  15.9 0.3 fusion.5
  16.3 1.1 %copy.98 = bf16[12,32,256]{0,2,1:T(8,128)(2,1)S(1)} copy(bf16[12,32,256]{2,0,1:T(8,128)(2,1)S(1)} %fusion.5) | data formatting | bytes 393216 | tf_op jit(solution)/shard_map/convert_element_type | solution.py:46
  17.3 1.3 %fusion.34 = bf16[1,24,16,128]{3,1,0,2:T(8,128)(2,1)} fusion(bf16[12,16,2,128,2]{0,4,3,2,1:T(2,128)(2,1)S(1)} %bitcast.423, f32[24]{0:T(128)S(1)} %copy-done.5, bf16[2,2,12,24]{3,1,0,2:T(2,128)(2,1)S(1)} %bitcast.424), kind=kOutput, calls=%fused_computation.62 | convolution fusion | flops 4866048 | bytes 297312 | tf_op jit(solution)/shard_map/zcxayb,abcd->zdxy/dot_general | solution.py:53
  18.7 5.5 %all-to-all-start = ((bf16[1,24,16,128]{3,1,0,2:T(8,128)(2,1)}), bf16[1,24,16,128]{3,1,0,2:T(8,128)(2,1)S(1)}, u32[]{:S(2)}, u32[]{:S(2)}) async-start(bf16[1,24,16,128]{3,1,0,2:T(8,128)(2,1)} %fusion.34), calls=%async_computation | async-start | bytes 196608 | tf_op jit(solution)/shard_map/all_to_all | solution.py:110
  24.2 0.8 %fusion.160 = (bf16[1,24,24]{0,2,1:T(8,128)(2,1)S(1)}, bf16[1,24,24]{0,2,1:T(8,128)(2,1)S(1)}, bf16[1,24,24]{0,2,1:T(8,128)(2,1)S(1)}, bf16[1,24,24]{0,2,1:T(8,1...) fusion(bf16[27,24,24]{0,2,1:T(8,128)(2,1)S(1)} %copy-done), kind=kLoop, calls=%fused_computation.212 | loop fusion | bytes 43776 | tf_op jit(solution)/shard_map/slice | solution.py:79
  25.0 5.2 %all-to-all-done = bf16[1,24,16,128]{3,1,0,2:T(8,128)(2,1)S(1)} async-done(((bf16[1,24,16,128]{3,1,0,2:T(8,128)(2,1)}), bf16[1,24,16,128]{3,1,0,2:T(8,128)(2,1)S(1)}, u32[]{:S(2)}, u32[]{:S(2)}) %all-to-all-start) | async-done | bytes 98336 | tf_op jit(solution)/shard_map/all_to_all | solution.py:110
  30.2 0.6 %fusion.162 = (bf16[8,24,1,128]{3,1,2,0:T(8,128)(2,1)}, bf16[8,24,1,128]{3,1,2,0:T(8,128)(2,1)}) fusion(bf16[8,24,2,128]{3,1,2,0:T(8,128)(2,1)S(1)} %bitcast.418), kind=kLoop, calls=%fused_computation.214 | loop fusion | bytes 196608 | tf_op jit(solution)/shard_map/slice | solution.py:12
  30.8 1.9 %collective-permute-start.2 = (bf16[8,24,1,128]{3,1,2,0:T(8,128)(2,1)}, bf16[8,24,1,128]{3,1,2,0:T(8,128)(2,1)S(1)}, u32[]{:S(2)}, u32[]{:S(2)}) collective-permute-start(bf16[8,24,1,128]{3,1,2,0:T(8,128)(2,1)} %get-tuple-element.32), channel_id=1, source_target_pairs={{0,1},{1,2},{2,3},{3,4},{4,5},{5,6},{6,7},{7,8},{8,9},{9,10},{10,1... | collective-permute-start | bytes 147464 | tf_op jit(solution)/shard_map/ppermute | solution.py:14
  32.7 6.3 %collective-permute-start.3 = (bf16[8,24,1,128]{3,1,2,0:T(8,128)(2,1)}, bf16[8,24,1,128]{3,1,2,0:T(8,128)(2,1)}, u32[]{:S(2)}, u32[]{:S(2)}) collective-permute-start(bf16[8,24,1,128]{3,1,2,0:T(8,128)(2,1)} %get-tuple-element.33), channel_id=1, source_target_pairs={{1,0},{2,1},{3,2},{4,3},{5,4},{6,5},{7,6},{8,7},{9,8},{10,9},{11,1... | collective-permute-start | bytes 147464 | tf_op jit(solution)/shard_map/ppermute | solution.py:15
  39.1 1.2 %fusion.161 = (bf16[1,24,24]{0,2,1:T(8,128)(2,1)}, bf16[1,24,24]{0,2,1:T(8,128)(2,1)}, bf16[1,24,24]{0,2,1:T(8,128)(2,1)}, bf16[1,24,24]{0,2,1:T(8,128)(2,1)}, b...) fusion(bf16[27,24,24]{0,2,1:T(8,128)(2,1)S(1)} %copy-done), kind=kLoop, calls=%fused_computation.213 | loop fusion | bytes 18432 | tf_op jit(solution)/shard_map/slice | solution.py:79
  40.3 1.1 %copy.174 = bf16[1,24,24]{1,2,0:T(8,128)(2,1)S(1)} copy(bf16[1,24,24]{0,2,1:T(8,128)(2,1)} %get-tuple-element.24) | data formatting | bytes 2304
  41.4 1.1 %copy.173 = bf16[1,24,24]{1,2,0:T(8,128)(2,1)S(1)} copy(bf16[1,24,24]{0,2,1:T(8,128)(2,1)} %get-tuple-element.25) | data formatting | bytes 2304
  42.5 1.1 %copy.172 = bf16[1,24,24]{1,2,0:T(8,128)(2,1)S(1)} copy(bf16[1,24,24]{0,2,1:T(8,128)(2,1)} %get-tuple-element.26) | data formatting | bytes 2304
  43.7 1.1 %copy.171 = bf16[1,24,24]{1,2,0:T(8,128)(2,1)S(1)} copy(bf16[1,24,24]{0,2,1:T(8,128)(2,1)} %get-tuple-element.27) | data formatting | bytes 2304
  44.8 1.1 %copy.170 = bf16[1,24,24]{1,2,0:T(8,128)(2,1)S(1)} copy(bf16[1,24,24]{0,2,1:T(8,128)(2,1)} %get-tuple-element.28) | data formatting | bytes 2304
  46.0 0.2 copy.169
  46.2 0.2 copy.168
  46.4 0.2 copy.167
  46.7 0.2 copy.193
  46.9 0.2 copy.192
  47.2 0.2 copy.191
  47.4 0.2 copy.190
  47.7 0.2 copy.189
  47.9 0.2 copy.188
  48.2 0.2 copy.187
  48.4 0.2 copy.186
  48.7 0.2 copy.185
  48.9 0.2 copy.184
  49.1 0.2 copy.183
  49.4 0.2 copy.182
  49.6 0.2 copy.181
  49.9 0.2 copy.180
  50.1 0.2 copy.179
  50.4 0.2 copy.178
  50.6 0.2 copy.177
  50.9 0.2 copy.176
  51.1 0.2 copy.175
  51.4 1.0 %select_maximum_fusion = bf16[10,24,4,130]{3,1,2,0:T(8,128)(2,1)S(1)} fusion(bf16[8,24,1,128]{3,1,2,0:T(8,128)(2,1)} %collective-permute-done.3, bf16[8,24,2,128]{3,1,2,0:T(8,128)(2,1)S(1)} %bitcast.419, bf16[8,24,1,128]{3,1,2,0:T(8,128)(2,1)S(1)} %collective-permute-done.2), kind=kLoop, calls=%fused_computation.73 | loop fusion | flops 2371200 | bytes 446208 | tf_op jit(solution)/shard_map/concatenate | solution.py:16
  53.4 0.2 convolution_add_fusion.20
  53.8 0.2 convolution_add_fusion.18
  54.0 0.2 convolution_add_fusion.17
  54.4 0.2 convolution_add_fusion.15
  55.8 1.0 %fusion.18 = f32[8,24,2,128]{3,1,2,0:T(8,128)S(1)} fusion(f32[8,24,2,128]{3,1,2,0:T(8,128)S(1)} %convolution_bitcast_fusion.9, f32[8,2,128,24]{2,3,1,0:T(8,128)S(1)} %convolution_add_fusion.10, bf16[8,24,1,128]{3,1,2,0:T(8,128)(2,1)} %collective-permute-done.3, bf16[8,24,2,128]{3,1,2,0:T(8,128)(2,1)S(1)} %bitcast.422, bf16[1,24,24]{1,2,0:T(8,128)(2,1)S(1)} %copy.183), kind=kOutput, calls=%fused_computation.54 | convolution fusion | flops 2752512 | bytes 738432 | tf_op jit(solution)/shard_map/zcxy,cd->zdxy/dot_general | solution.py:76
  56.9 0.2 fusion.7
  57.1 0.2 fusion.8
  57.5 0.2 fusion.10
  57.8 0.2 fusion.11
  58.4 0.2 fusion.33
  58.6 0.7 %copy.129 = bf16[8,24,2,128]{3,2,1,0:T(2,128)(2,1)} copy(bf16[8,24,2,128]{3,1,2,0:T(8,128)(2,1)S(1)} %fusion.33) | data formatting | bytes 196608 | tf_op jit(solution)/shard_map/convert_element_type | solution.py:82
  (34 shorter events, 3.2 us)
Async XLA Ops:
  0.0 14.1 %copy-start.1 = (bf16[9,12,12]{2,1,0:T(8,128)(2,1)S(1)}, bf16[9,12,12]{2,1,0:T(8,128)(2,1)}, u32[]{:S(2)}) copy-start(bf16[9,12,12]{2,1,0:T(8,128)(2,1)} %param.12) | copy-start | bytes 7780
  0.7 7.5 %collective-permute-start = (bf16[1,2,256]{2,1,0:T(2,128)(2,1)S(1)}, bf16[1,2,256]{2,1,0:T(2,128)(2,1)S(1)}, u32[]{:S(2)}, u32[]{:S(2)}) collective-permute-start(bf16[1,2,256]{2,1,0:T(2,128)(2,1)S(1)} %get-tuple-element.43), channel_id=1, source_target_pairs={{0,8},{8,16},{16,24},{1,9},{9,17},{17,25},{2,10},{10,18},{18,26},{... | collective-permute-start | bytes 3080 | tf_op jit(solution)/shard_map/ppermute | solution.py:14
  5.3 4.9 %collective-permute-start.1 = (bf16[1,2,256]{2,1,0:T(2,128)(2,1)S(1)}, bf16[1,2,256]{2,1,0:T(2,128)(2,1)S(1)}, u32[]{:S(2)}, u32[]{:S(2)}) collective-permute-start(bf16[1,2,256]{2,1,0:T(2,128)(2,1)S(1)} %get-tuple-element.44), channel_id=1, source_target_pairs={{8,0},{16,8},{24,16},{9,1},{17,9},{25,17},{10,2},{18,10},{26,18},{... | collective-permute-start | bytes 3080 | tf_op jit(solution)/shard_map/ppermute | solution.py:15
  15.0 0.9 %copy-start.2 = (f32[12]{0:T(128)S(1)}, f32[12]{0:T(128)}, u32[]{:S(2)}) copy-start(f32[12]{0:T(128)} %param.13) | copy-start | bytes 148
  15.6 1.7 %copy-start.4 = (bf16[4,12,24]{2,0,1:T(4,128)(2,1)S(1)}, bf16[4,12,24]{2,0,1:T(4,128)(2,1)}, u32[]{:S(2)}) copy-start(bf16[4,12,24]{2,0,1:T(4,128)(2,1)} %param.14) | copy-start | bytes 6916
  15.6 1.7 %copy-start.5 = (f32[24]{0:T(128)S(1)}, f32[24]{0:T(128)}, u32[]{:S(2)}) copy-start(f32[24]{0:T(128)} %param.15) | copy-start | bytes 292
  16.2 7.9 %copy-start = (bf16[27,24,24]{0,2,1:T(8,128)(2,1)S(1)}, bf16[27,24,24]{0,2,1:T(8,128)(2,1)}, u32[]{:S(2)}) copy-start(bf16[27,24,24]{0,2,1:T(8,128)(2,1)} %param.16) | copy-start | bytes 93316
  18.7 11.5 %all-to-all-start = ((bf16[1,24,16,128]{3,1,0,2:T(8,128)(2,1)}), bf16[1,24,16,128]{3,1,0,2:T(8,128)(2,1)S(1)}, u32[]{:S(2)}, u32[]{:S(2)}) async-start(bf16[1,24,16,128]{3,1,0,2:T(8,128)(2,1)} %fusion.34), calls=%async_computation | async-start | bytes 196608 | tf_op jit(solution)/shard_map/all_to_all | solution.py:110
  30.8 20.6 %collective-permute-start.2 = (bf16[8,24,1,128]{3,1,2,0:T(8,128)(2,1)}, bf16[8,24,1,128]{3,1,2,0:T(8,128)(2,1)S(1)}, u32[]{:S(2)}, u32[]{:S(2)}) collective-permute-start(bf16[8,24,1,128]{3,1,2,0:T(8,128)(2,1)} %get-tuple-element.32), channel_id=1, source_target_pairs={{0,1},{1,2},{2,3},{3,4},{4,5},{5,6},{6,7},{7,8},{8,9},{9,10},{10,1... | collective-permute-start | bytes 147464 | tf_op jit(solution)/shard_map/ppermute | solution.py:14
  32.7 18.6 %collective-permute-start.3 = (bf16[8,24,1,128]{3,1,2,0:T(8,128)(2,1)}, bf16[8,24,1,128]{3,1,2,0:T(8,128)(2,1)}, u32[]{:S(2)}, u32[]{:S(2)}) collective-permute-start(bf16[8,24,1,128]{3,1,2,0:T(8,128)(2,1)} %get-tuple-element.33), channel_id=1, source_target_pairs={{1,0},{2,1},{3,2},{4,3},{5,4},{6,5},{7,6},{8,7},{9,8},{10,9},{11,1... | collective-permute-start | bytes 147464 | tf_op jit(solution)/shard_map/ppermute | solution.py:15
  56.7 1.7 %copy-start.3 = (f32[24]{0:T(128)S(1)}, f32[24]{0:T(128)}, u32[]{:S(2)}) copy-start(f32[24]{0:T(128)} %param.17) | copy-start | bytes 292
where the time goes:
time: 60.1 us; the launch traced here: 59.4 us
  starting transfers between devices  20.2 us (34%)
  local copies, waits for them, and re-layouts  16.2 us (27%)
  matrix products  11.4 us (19%)
  waiting for transfers between devices  7.12 us (12%)
  other arithmetic  3.94 us (7%)
    unnamed x39, local copies, waits for them, and re-layouts  11.1 us
    ppermute x2, starting transfers between devices, extended(): after = lax.ppermute(first, axis, down)  8.25 us
    ppermute x2, starting transfers between devices, extended(): before = lax.ppermute(last, axis, up)  6.44 us
    dot_general x27, matrix products, deep_conv(): jnp.einsum('zcxy,cd->zdxy', window, deep_weight[9 * along_z + 3 * along_x...  6.02 us
    all_to_all x1, starting transfers between devices, shards(): lax.all_to_all(resident_reduced, 'zs', split_axis=2, concat_axis=0, tiled...  5.53 us
    all_to_all x1, waiting for transfers between devices, shards(): lax.all_to_all(resident_reduced, 'zs', split_axis=2, concat_axis=0, tiled...  5.17 us
    dot_general x9, matrix products, plane_conv(): jnp.einsum('zcxy,cd->zdxy', window, weight[3 * along_x + along_y], prefer...  4.05 us
    slice x2, local copies, waits for them, and re-layouts, deep_conv(): deep_weight[9 * along_z + 3 * along_x + along_y]  2 us
  transfers between devices with their start and end apart: 5, of which 2 were waited for; matrix products, arithmetic and copies ran while one was open for 24% of the time, Pallas kernels for 0%

commit v1 on v0

v1 whole, which is shorter than its diff:
```python
import functools

import jax
import jax.numpy as jnp
from jax import lax
from jax.experimental import pallas as pl
from jax.experimental.pallas import tpu as pltpu
from jax.sharding import PartitionSpec as P

TILE = 16
SHIFTS = ((1, 2, 0, None), (0, 1, None, 2))
F32 = jnp.float32
BF16 = jnp.bfloat16


def iota(shape, dim):
    return lax.broadcasted_iota(jnp.int32, shape, dim)


def ceil_to(value, step):
    return -(-value // step) * step


def div(value, by):
    if by & (by - 1) == 0:
        return lax.shift_right_logical(value, by.bit_length() - 1)
    return lax.shift_right_logical(value * (-(-65536 // by)), 16)


def one_hot(condition):
    return jnp.where(condition, 1.0, 0.0).astype(BF16)


def nt_dot(lhs, rhs):
    return lax.dot_general(lhs, rhs, (((1,), (1,)), ((), ())), preferred_element_type=F32)


def nn_dot(lhs, rhs):
    return jnp.dot(lhs, rhs, preferred_element_type=F32)


class Sizes:
    def __init__(self, volume, first_weight, reduce_conv_weight, vols, members):
        self.depth = volume.shape[0] * members
        self.cols = volume.shape[2]
        self.half = self.cols // 2
        self.fine_rows = volume.shape[1] * vols
        self.rows = volume.shape[1]
        self.strip = volume.shape[1] // 2 // members
        self.chan = first_weight.shape[1]
        self.deep = reduce_conv_weight.shape[2]
        self.coarse_rows = self.strip + 2
        self.second_rows = 2 * self.coarse_rows
        self.first_rows = self.second_rows + 2
        self.window = self.first_rows + 2
        self.pieces = self.window // 4
        self.lines = ceil_to(self.window, TILE)
        self.ones1 = self.first_rows * self.chan
        self.m1 = ceil_to(self.ones1 + 3, TILE)
        self.m2 = self.second_rows * self.chan
        self.m3 = self.coarse_rows * self.deep
        self.m4 = self.strip * self.deep

    def base(self, member):
        return 2 * self.strip * member - 4


def sort_kernel(z, own_ref, sort_ref, sorted_ref):
    core = lax.rem(lax.axis_index("vol"), 2)
    shape = (z.cols, z.half)
    sort = one_hot(iota(shape, 0) == 2 * iota(shape, 1) + core)
    sort_ref[...] = sort
    for s in range(own_ref.shape[0]):
        sorted_ref[s] = nn_dot(own_ref[s], sort)


def pack_kernel(z, chips, members, own_ref, sort_ref, other_ref, packed_ref):
    vol = lax.axis_index("vol")
    chip = lax.div(vol, 2)
    first_core = vol - 2 * chip == 0
    packed_ref[...] = jnp.zeros(packed_ref.shape, BF16)
    slices = own_ref.shape[0]
    empty = jnp.zeros((4, z.half), BF16)
    for s in range(slices):
        own, other = own_ref[s], nn_dot(other_ref[s], sort_ref[...])
        lines = stacked([jnp.where(first_core, own, other), jnp.where(first_core, other, own)])
        pieces = [lines[row : row + 4].astype(BF16) for row in range(0, 2 * z.rows, 4)]

        def put(to, first):
            for piece in range(z.pieces):
                at = first // 4 + piece
                value = pieces[at] if 0 <= at < len(pieces) else empty
                packed_ref[(to * slices + s) * z.pieces + piece] = value

        for core in range(2):
            for member in range(members):
                put((2 * chip + core) * members + member, core * z.rows + z.base(member))

        @pl.when(chip < chips - 1)
        def _():
            put(2 * (chip + 1) * members, 2 * z.rows - 4)

        @pl.when(chip > 0)
        def _():
            put(2 * chip * members - 1, 4 - z.window)


def prepare_kernel(
    z, members, w1_ref, b1_ref, w2_ref, b2_ref, w3_ref, b3_ref, w4_ref, b4_ref,
    k1_ref, k2_ref, k3_ref, k4_ref,
):
    member = lax.axis_index("zs")
    start = (lax.axis_index("vol") * members + member) * (2 * z.strip)
    def spread(rows, offsets, period, stretch):
        row = div(iota((rows, period), 0), stretch)
        at = row - div(row, period) * period
        picked = jnp.where(at == iota((rows, period), 1), offsets, 0.0)
        return jnp.sum(picked, axis=1, keepdims=True)

    def bias_terms(column, at):
        high = column.astype(BF16).astype(F32)
        middle = (column - high).astype(BF16).astype(F32)
        low = column - high - middle
        return jnp.where(at == 0, high, jnp.where(at == 1, middle, jnp.where(at == 2, low, 0.0)))

    row = iota((z.m1, z.chan), 0)
    pick = one_hot(row - div(row, z.chan) * z.chan == iota((z.m1, z.chan), 1))
    taps = nt_dot(pick, w1_ref[...]).astype(BF16)
    shape = (z.m1, 4 * z.lines)
    x = div(iota(shape, 0), z.chan)
    col = iota(shape, 1)
    line = col - div(col, z.lines) * z.lines
    inside = (start - 3 + x >= 0) & (start - 3 + x < z.fine_rows) & (x < z.first_rows)
    block = div(iota((9, 4 * z.lines), 1), z.lines)
    narrow = (z.m1, TILE)
    row, col = iota(narrow, 0), iota(narrow, 1)
    narrow_x = div(row, z.chan)
    narrow_inside = (start - 3 + narrow_x >= 0) & (start - 3 + narrow_x < z.fine_rows)
    bias = jnp.where(narrow_inside, bias_terms(spread(z.m1, b1_ref[...], z.chan, 1), col), 0.0)
    ones = jnp.where((row < z.ones1 + 3) & (col == 0), 1.0, 0.0)
    bias = jnp.where(row < z.ones1, bias, ones).astype(BF16)
    for parity, shifts in enumerate(SHIFTS):
        shift = jnp.full(block.shape, 9, jnp.int32)
        for number, value in enumerate(shifts):
            if value is not None:
                shift = jnp.where(block == number, value, shift)
        total = jnp.zeros(shape, F32)
        for i in range(3):
            level = nn_dot(taps, one_hot(iota(block.shape, 0) == 3 * i + shift))
            total += jnp.where(inside & (line == x + i), level, 0.0)
        k1_ref[parity * z.m1 : (parity + 1) * z.m1, : 4 * z.lines] = total.astype(BF16)
        k1_ref[parity * z.m1 : (parity + 1) * z.m1, 4 * z.lines :] = bias

    row = iota((z.m2, z.chan), 0)
    pick = one_hot(row - div(row, z.chan) * z.chan == iota((z.m2, z.chan), 1))
    col = iota((z.chan, z.m1), 1)
    widen = one_hot(col - div(col, z.chan) * z.chan == iota((z.chan, z.m1), 0))
    shape = (z.m2, z.m1)
    lag = div(iota(shape, 1), z.chan) - div(iota(shape, 0), z.chan)
    bias = bias_terms(spread(z.m2, b2_ref[...], z.chan, 1), iota(shape, 1) - z.ones1)
    for s in range(3):
        total = bias if s == 1 else jnp.zeros(shape, F32)
        for i in range(3):
            level = nn_dot(nt_dot(pick, w2_ref[3 * i + s]).astype(BF16), widen)
            total += jnp.where(lag == i, level, 0.0)
        total = total.astype(BF16)
        for parity, shifts in enumerate(SHIFTS):
            at = shifts.index(s)
            k2_ref[parity * z.m2 : (parity + 1) * z.m2, at * z.m1 : (at + 1) * z.m1] = total
    for parity, shifts in enumerate(SHIFTS):
        at = shifts.index(None)
        k2_ref[parity * z.m2 : (parity + 1) * z.m2, at * z.m1 : (at + 1) * z.m1] = jnp.zeros(shape, BF16)

    row = iota((z.m3, z.deep), 0)
    u = div(row, z.deep)
    pick = one_hot(row - u * z.deep == iota((z.m3, z.deep), 1))
    col = iota((z.chan, z.m2), 1)
    widen = one_hot(col - div(col, z.chan) * z.chan == iota((z.chan, z.m2), 0))
    shape = (z.m3, z.m2)
    u = div(iota(shape, 0), z.deep)
    lag = div(iota(shape, 1), z.chan) - 2 * u
    inside = (start + 2 * u >= 2) & (start + 2 * u < z.fine_rows + 2)
    for b in range(2):
        total = jnp.zeros(shape, F32)
        for a in range(2):
            level = nn_dot(nt_dot(pick, w3_ref[2 * a + b]).astype(BF16), widen)
            total += jnp.where(inside & (lag == a), level, 0.0)
        k3_ref[:, b * z.m2 : (b + 1) * z.m2] = total.astype(BF16)
    shape = (z.m3, TILE)
    u = div(iota(shape, 0), z.deep)
    inside = (start + 2 * u >= 2) & (start + 2 * u < z.fine_rows + 2)
    bias = bias_terms(spread(z.m3, b3_ref[...], z.deep, 1), iota(shape, 1))
    k3_ref[:, 2 * z.m2 :] = jnp.where(inside, bias, 0.0).astype(BF16)

    row = iota((z.m4, z.deep), 0)
    pick = one_hot(div(row, z.strip) == iota((z.m4, z.deep), 1))
    col = iota((z.deep, z.m3), 1)
    widen = one_hot(col - div(col, z.deep) * z.deep == iota((z.deep, z.m3), 0))
    shape = (z.m4, z.m3)
    row = iota(shape, 0)
    lag = div(iota(shape, 1), z.deep) - (row - div(row, z.strip) * z.strip)
    for i in range(3):
        for s in range(3):
            total = jnp.zeros(shape, F32)
            for j in range(3):
                level = nn_dot(nt_dot(pick, w4_ref[9 * i + 3 * j + s]).astype(BF16), widen)
                total += jnp.where(lag == j, level, 0.0)
            k4_ref[i * z.m4 : (i + 1) * z.m4, s * z.m3 : (s + 1) * z.m3] = total.astype(BF16)
    shape = (z.m4, TILE)
    bias = bias_terms(spread(z.m4, b4_ref[...], z.deep, z.strip), iota(shape, 1))
    for i in range(3):
        terms = bias if i == 1 else jnp.zeros(shape, F32)
        k4_ref[i * z.m4 : (i + 1) * z.m4, 3 * z.m3 :] = terms.astype(BF16)


def relu(value):
    return jnp.maximum(value.astype(BF16), 0)


def side_by_side(values):
    return jnp.concatenate(values, axis=1)


def stacked(values):
    return jnp.concatenate(values, axis=0)


def moved(value, by, lanes):
    width = value.shape[1]
    turned = pltpu.roll(value, by % width, axis=1)
    edge = 0 if by == 1 else width - 1
    return jnp.where(lanes == edge, jnp.zeros_like(turned), turned)


def main_kernel(
    z, chips, got_ref, k1_ref, k2_ref, k3_ref, k4_ref, out_ref, coarse,
):
    chip = lax.div(lax.axis_index("vol"), 2)
    sources = [chip]
    if chips > 1:
        sources.append(lax.rem(chip + 1, chips))
    if chips > 2:
        sources.append(lax.rem(chip + chips - 1, chips))
    group = min(z.depth, 8)
    groups = z.depth // group
    n = z.half
    ones = jnp.ones((TILE, group * n), BF16)
    blanks = [jnp.zeros((z.lines - z.window, n), F32)] if z.lines > z.window else []
    lanes0 = iota((z.lines, n), 1)
    lanes1 = iota((z.m1, n), 1)
    lanes3 = iota((z.m3, n), 1)
    if groups > 1:
        coarse[0] = jnp.zeros((z.m3, n), BF16)
        coarse[z.depth + 1] = jnp.zeros((z.m3, n), BF16)

    def blocks(evens, odds, lanes):
        odds_right = [moved(odd, 1, lanes) for odd in odds]
        evens_left = [moved(even, -1, lanes) for even in evens]
        return [side_by_side(pair) for pair in (evens, odds, odds_right, evens_left)]

    def lines_of(k, core):
        pieces = []
        for piece in range(z.pieces):
            at = k * z.pieces + piece
            pieces.append(sum(got_ref[source, core, at].astype(F32) for source in sources))
        return stacked(pieces + blanks)

    def split(value):
        return [value[:, k : k + n] for k in range(0, value.shape[1], n)]

    def leading(base):
        evens, odds = ([lines_of(base + k, core) for k in range(group)] for core in range(2))
        field = stacked([stacked(blocks(evens, odds, lanes0)).astype(BF16), ones])
        first = relu(nn_dot(k1_ref[...], field))
        moves = blocks(split(first[: z.m1]), split(first[z.m1 :]), lanes1)[2:]
        second = relu(nn_dot(k2_ref[...], stacked([first] + moves)))
        reduced = relu(nn_dot(k3_ref[...], stacked([second, ones])))
        for k, plane in enumerate(split(reduced)):
            coarse[base + k + 1] = plane

    def trailing(base):
        around = list(range(-1, group + 1)) if groups > 1 else list(range(group))
        planes = [coarse[base + k + 1] for k in around]
        field = stacked([
            side_by_side([moved(plane, 1, lanes3) for plane in planes]),
            side_by_side(planes),
            side_by_side([moved(plane, -1, lanes3) for plane in planes]),
            jnp.ones((TILE, len(planes) * n), BF16),
        ])
        terms = split(nn_dot(k4_ref[...], field))
        for k in range(group):
            parts = [
                terms[around.index(k + i - 1)][i * z.m4 : (i + 1) * z.m4] for i in range(3) if k + i - 1 in around
            ]
            out_ref[base + k] = relu(sum(parts[1:], parts[0]))

    if groups == 1:
        leading(0)
        trailing(0)
    else:
        pl.loop(0, groups)(lambda g: leading(g * group))
        pl.loop(0, groups)(lambda g: trailing(g * group))


def shards(
    volume, first_weight, first_offset, second_weight, second_offset,
    reduce_conv_weight, reduce_conv_bias, deep_weight, deep_offset,
):
    vols, members = lax.axis_size("vol"), lax.axis_size("zs")
    z = Sizes(volume, first_weight, reduce_conv_weight, vols, members)
    slices = volume.shape[0]
    vmem = pl.BlockSpec(memory_space=pltpu.VMEM)
    like = jax.ShapeDtypeStruct
    chips = vols // 2
    other = lax.ppermute(volume, "vol", [(v, v ^ 1) for v in range(vols)])
    sort, own = pl.pallas_call(
        functools.partial(sort_kernel, z),
        out_shape=(like((z.cols, z.half), BF16), like((slices, z.rows, z.half), F32)),
        in_specs=[vmem],
        out_specs=(vmem,) * 2,
        compiler_params=pltpu.CompilerParams(vmem_limit_bytes=16 * 1024 * 1024),
        cost_estimate=pl.CostEstimate(flops=5_000_000, bytes_accessed=100_000, transcendentals=0),
        name="sort",
    )(volume)
    packed = pl.pallas_call(
        functools.partial(pack_kernel, z, chips, members),
        out_shape=like((vols * members * slices * z.pieces, 4, z.half), BF16),
        in_specs=[vmem] * 3,
        out_specs=vmem,
        compiler_params=pltpu.CompilerParams(vmem_limit_bytes=16 * 1024 * 1024),
        name="pack",
    )(own, sort, other)
    packed, *parameters = lax.optimization_barrier((
        packed, first_weight, first_offset, second_weight, second_offset,
        reduce_conv_weight, reduce_conv_bias, deep_weight, deep_offset,
    ))
    got = lax.all_to_all(packed, ("vol", "zs"), split_axis=0, concat_axis=0, tiled=True)
    got = got.reshape(chips, 2, z.depth * z.pieces, 4, z.half)
    prepared = pl.pallas_call(
        functools.partial(prepare_kernel, z, members),
        out_shape=(
            like((2 * z.m1, 4 * z.lines + TILE), BF16),
            like((2 * z.m2, 4 * z.m1), BF16),
            like((z.m3, 2 * z.m2 + TILE), BF16),
            like((3 * z.m4, 3 * z.m3 + TILE), BF16),
        ),
        in_specs=[vmem] * 8,
        out_specs=(vmem,) * 4,
        compiler_params=pltpu.CompilerParams(vmem_limit_bytes=16 * 1024 * 1024),
        cost_estimate=pl.CostEstimate(flops=50_000_000, bytes_accessed=1_000_000, transcendentals=0),
        name="prepare",
    )(
        *(value[None] if value.ndim == 1 else value for value in parameters)
    )
    affinity = pl.pallas_call(
        functools.partial(main_kernel, z, chips),
        out_shape=like((z.depth, z.m4, z.half), BF16),
        in_specs=[vmem] * 5,
        out_specs=vmem,
        scratch_shapes=[
            pltpu.VMEM((z.depth + 2, z.m3, z.half), BF16),
        ],
        compiler_params=pltpu.CompilerParams(vmem_limit_bytes=32 * 1024 * 1024),
        cost_estimate=pl.CostEstimate(flops=2_000_000_000, bytes_accessed=2_000_000, transcendentals=0),
        name="encode",
    )(got, *prepared)
    return affinity.reshape(z.depth, z.deep, z.strip, z.half)


def solution(mesh):
    return jax.shard_map(
        shards,
        mesh=mesh,
        in_specs=(P("zs", "vol", None), P(), P(), P(), P(), P(), P(), P(), P()),
        out_specs=P(None, None, ("vol", "zs"), None),
        check_vma=False,
    )
```

time: 60.1 us -> 19.2 us (0.32)
  the two profiles are of different devices: /device:TPU:1 before, /device:TPU:0 now
where the time goes in v1:
time: 19.2 us; the launch traced here: 18.9 us
  starting transfers between devices  7.64 us (40%)
  waiting for transfers between devices  5.62 us (29%)
  Pallas kernels  3.86 us (20%)
  local copies, waits for them, and re-layouts  1.68 us (9%)
    all_to_all x1, starting transfers between devices, shards(): lax.all_to_all(packed, ('vol', 'zs'), split_axis=0, concat_axis=0, tiled=...  7.19 us
    all_to_all x1, waiting for transfers between devices, shards(): lax.all_to_all(packed, ('vol', 'zs'), split_axis=0, concat_axis=0, tiled=...  5.42 us
    pallas_call x1, Pallas kernels, shards(): pl.pallas_call(functools.partial(main_kernel, z, chips), out_shape=like((...  1.84 us
    unnamed x18, local copies, waits for them, and re-layouts  1.41 us
    pallas_call x1, Pallas kernels, shards(): pl.pallas_call(functools.partial(prepare_kernel, z, members), out_shape=(...  1.1 us
    pallas_call x1, Pallas kernels, shards(): pl.pallas_call(functools.partial(pack_kernel, z, chips, members), out_sha...  0.79 us
    ppermute x1, starting transfers between devices, shards(): other = lax.ppermute(volume, 'vol', [(v, v ^ 1) for v in range(vols)])  0.45 us
  transfers between devices with their start and end apart: 2, of which 2 were waited for; matrix products, arithmetic and copies ran while one was open for 1% of the time, Pallas kernels for 7%

profile of v1, /device:TPU:0, one launch (start us, length us, event | category | flops | bytes accessed | tf_op | source)
XLA Modules:
  0.0 18.9 jit_solution(1832652672343296662)
XLA Ops:
  0.0 0.5 %collective-permute-start = (bf16[1,32,256]{2,1,0:T(8,128)(2,1)}, bf16[1,32,256]{2,1,0:T(8,128)(2,1)S(1)}, u32[]{:S(2)}, u32[]{:S(2)}) collective-permute-start(bf16[1,32,256]{2,1,0:T(8,128)(2,1)} %own_ref.1), channel_id=1, source_target_pairs={{0,8},{8,0},{16,24},{24,16},{1,9},{9,1},{17,25},{25,17},{2,10},{10... | collective-permute-start | bytes 49160 | tf_op jit(solution)/shard_map/ppermute | solution.py:315
  0.5 0.0 copy-start.6
  0.5 0.7 %copy-done.6 = bf16[1,32,256]{2,1,0:T(8,128)(2,1)S(1)} copy-done((bf16[1,32,256]{2,1,0:T(8,128)(2,1)S(1)}, bf16[1,32,256]{2,1,0:T(8,128)(2,1)}, u32[]{:S(2)}) %copy-start.6) | copy-done | bytes 16408
  1.2 0.1 sort.1
  1.3 0.2 %collective-permute-done.other_ref = bf16[1,32,256]{2,1,0:T(8,128)(2,1)S(1)} collective-permute-done((bf16[1,32,256]{2,1,0:T(8,128)(2,1)}, bf16[1,32,256]{2,1,0:T(8,128)(2,1)S(1)}, u32[]{:S(2)}, u32[]{:S(2)}) %collective-permute-start) | collective-permute-done | bytes 16416 | tf_op jit(solution)/shard_map/ppermute | solution.py:315
  1.5 0.8 %pack.1 = bf16[96,4,128]{2,1,0:T(4,128)(2,1)} custom-call(f32[1,32,128]{2,1,0:T(8,128)S(1)} %get-tuple-element.20.own_ref, bf16[256,128]{1,0:T(8,128)(2,1)S(1)} %get-tuple-element.21.sort_ref, bf16[1,32,256]{2,1,0:T(8,128)(2,1)S(1)} %collective-permute-done.other_ref), custom_call_target="tpu_custom_call" | custom-call | tf_op jit(solution)/shard_map/pack/pallas_call | solution.py:325
  2.3 0.0 copy-start.8
  2.3 0.0 copy-start.7
  2.3 7.2 %all-to-all-start = ((bf16[96,4,128]{2,1,0:T(4,128)(2,1)}), bf16[96,4,128]{2,1,0:T(4,128)(2,1)S(1)}, u32[]{:S(2)}, u32[]{:S(2)}) async-start(bf16[96,4,128]{2,1,0:T(4,128)(2,1)} %pack.1), calls=%async_computation | async-start | bytes 196608 | tf_op jit(solution)/shard_map/all_to_all | solution.py:337
  9.5 0.0 copy-done.8
  9.5 0.0 copy-done.7
  9.5 0.0 copy-start
  9.5 0.0 copy-start.5
  9.6 0.3 %copy.11.w4_ref = bf16[27,24,24]{2,1,0:T(8,128)(2,1)S(1)} copy(bf16[27,24,24]{0,2,1:T(8,128)(2,1)S(1)} %copy-done.7) | data formatting | bytes 62208 | tf_op jit(solution)/shard_map/optimization_barrier | solution.py:333
  9.8 0.0 copy-start.1
  9.8 0.0 copy-start.2
  9.8 0.0 copy-start.3
  9.8 0.0 copy-start.4
  9.9 0.4 %copy-done = bf16[9,12,12]{2,1,0:T(8,128)(2,1)S(1)} copy-done((bf16[9,12,12]{2,1,0:T(8,128)(2,1)S(1)}, bf16[9,12,12]{2,1,0:T(8,128)(2,1)}, u32[]{:S(2)}) %copy-start) | copy-done | bytes 2616
  10.3 0.0 copy-done.5
  10.3 0.2 %copy-done.1 = bf16[9,12]{1,0:T(8,128)(2,1)S(1)} copy-done((bf16[9,12]{1,0:T(8,128)(2,1)S(1)}, bf16[9,12]{1,0:T(8,128)(2,1)}, u32[]{:S(2)}) %copy-start.1) | copy-done | bytes 240
  10.5 0.0 copy-done.2
  10.5 0.0 copy-done.3
  10.5 0.0 copy-done.4
  10.5 1.1 %prepare.1 = (bf16[256,80]{1,0:T(8,128)(2,1)S(1)}, bf16[192,512]{1,0:T(8,128)(2,1)S(1)}, bf16[96,208]{1,0:T(8,128)(2,1)S(1)}, bf16[144,304]{1,0:T(8,128)(2,1)S(1)}) custom-call(bf16[9,12]{1,0:T(8,128)(2,1)S(1)} %copy-done.1, f32[1,12]{1,0:T(1,128)S(1)} %bitcast.7, bf16[9,12,12]{2,1,0:T(8,128)(2,1)S(1)} %copy-done, f32[1,12]{1,0:T(1,128)S(1)} %bitcast.8, ...), custom_call_target="tpu_custom_call" | custom-call | flops 50000000 | bytes 1000000 | tf_op jit(solution)/shard_map/prepare/pallas_call | solution.py:339
  11.6 5.4 %all-to-all-done = bf16[96,4,128]{2,1,0:T(4,128)(2,1)S(1)} async-done(((bf16[96,4,128]{2,1,0:T(4,128)(2,1)}), bf16[96,4,128]{2,1,0:T(4,128)(2,1)S(1)}, u32[]{:S(2)}, u32[]{:S(2)}) %all-to-all-start) | async-done | bytes 98336 | tf_op jit(solution)/shard_map/all_to_all | solution.py:337
  17.1 1.8 %encode.1 = bf16[8,48,128]{2,1,0:T(8,128)(2,1)} custom-call(bf16[2,2,24,4,128]{4,3,2,1,0:T(4,128)(2,1)S(1)} %bitcast.6, bf16[256,80]{1,0:T(8,128)(2,1)S(1)} %get-tuple-element.31.k1_ref, bf16[192,512]{1,0:T(8,128)(2,1)S(1)} %get-tuple-element.32.k2_ref, bf16[96,208]{1,0:T(8,128)(2,1)S(1)} %get-tuple-element.33.k3_ref, ...), custom_call_target="tpu_custom_call" | custom-call | flops 2000000000 | bytes 2000000 | tf_op jit(solution)/shard_map/encode/pallas_call | solution.py:355
  (1 shorter events, 0.0 us)
Async XLA Ops:
  0.0 1.5 %collective-permute-start = (bf16[1,32,256]{2,1,0:T(8,128)(2,1)}, bf16[1,32,256]{2,1,0:T(8,128)(2,1)S(1)}, u32[]{:S(2)}, u32[]{:S(2)}) collective-permute-start(bf16[1,32,256]{2,1,0:T(8,128)(2,1)} %own_ref.1), channel_id=1, source_target_pairs={{0,8},{8,0},{16,24},{24,16},{1,9},{9,1},{17,25},{25,17},{2,10},{10... | collective-permute-start | bytes 49160 | tf_op jit(solution)/shard_map/ppermute | solution.py:315
  0.5 0.7 %copy-start.6 = (bf16[1,32,256]{2,1,0:T(8,128)(2,1)S(1)}, bf16[1,32,256]{2,1,0:T(8,128)(2,1)}, u32[]{:S(2)}) copy-start(bf16[1,32,256]{2,1,0:T(8,128)(2,1)} %own_ref.1) | copy-start | bytes 49156
  2.3 7.2 %copy-start.8 = (bf16[4,12,24]{2,0,1:T(4,128)(2,1)S(1)}, bf16[4,12,24]{2,0,1:T(4,128)(2,1)}, u32[]{:S(2)}) copy-start(bf16[4,12,24]{2,0,1:T(4,128)(2,1)} %param.14) | copy-start | bytes 6916
  2.3 7.2 %copy-start.7 = (bf16[27,24,24]{0,2,1:T(8,128)(2,1)S(1)}, bf16[27,24,24]{0,2,1:T(8,128)(2,1)}, u32[]{:S(2)}) copy-start(bf16[27,24,24]{0,2,1:T(8,128)(2,1)} %param.16) | copy-start | bytes 93316
  2.3 14.8 %all-to-all-start = ((bf16[96,4,128]{2,1,0:T(4,128)(2,1)}), bf16[96,4,128]{2,1,0:T(4,128)(2,1)S(1)}, u32[]{:S(2)}, u32[]{:S(2)}) async-start(bf16[96,4,128]{2,1,0:T(4,128)(2,1)} %pack.1), calls=%async_computation | async-start | bytes 196608 | tf_op jit(solution)/shard_map/all_to_all | solution.py:337
  9.5 0.8 %copy-start = (bf16[9,12,12]{2,1,0:T(8,128)(2,1)S(1)}, bf16[9,12,12]{2,1,0:T(8,128)(2,1)}, u32[]{:S(2)}) copy-start(bf16[9,12,12]{2,1,0:T(8,128)(2,1)} %w2_ref) | copy-start | bytes 7780
  9.5 0.8 %copy-start.5 = (f32[24]{0:T(128)S(1)}, f32[24]{0:T(128)}, u32[]{:S(2)}) copy-start(f32[24]{0:T(128)} %param.17) | copy-start | bytes 292
  9.8 0.7 %copy-start.1 = (bf16[9,12]{1,0:T(8,128)(2,1)S(1)}, bf16[9,12]{1,0:T(8,128)(2,1)}, u32[]{:S(2)}) copy-start(bf16[9,12]{1,0:T(8,128)(2,1)} %w1_ref) | copy-start | bytes 652
  9.8 0.7 %copy-start.2 = (f32[12]{0:T(128)S(1)}, f32[12]{0:T(128)}, u32[]{:S(2)}) copy-start(f32[12]{0:T(128)} %param.11) | copy-start | bytes 148
  9.8 0.7 %copy-start.3 = (f32[12]{0:T(128)S(1)}, f32[12]{0:T(128)}, u32[]{:S(2)}) copy-start(f32[12]{0:T(128)} %param.13) | copy-start | bytes 148
  9.8 0.7 %copy-start.4 = (f32[24]{0:T(128)S(1)}, f32[24]{0:T(128)}, u32[]{:S(2)}) copy-start(f32[24]{0:T(128)} %param.15) | copy-start | bytes 292

commit v2 on v1

--- a/solution.py
+++ b/solution.py
@@ -90,7 +90,7 @@
             for piece in range(z.pieces):
                 at = first // 4 + piece
                 value = pieces[at] if 0 <= at < len(pieces) else empty
-                packed_ref[(to * slices + s) * z.pieces + piece] = value
+                packed_ref[to * slices + s, :, piece * z.half : (piece + 1) * z.half] = value
 
         for core in range(2):
             for member in range(members):
@@ -244,7 +244,7 @@
     group = min(z.depth, 8)
     groups = z.depth // group
     n = z.half
-    ones = jnp.ones((TILE, group * n), BF16)
+    ones = jnp.ones((TILE, z.cols), BF16)
     blanks = [jnp.zeros((z.lines - z.window, n), F32)] if z.lines > z.window else []
     lanes0 = iota((z.lines, n), 1)
     lanes1 = iota((z.m1, n), 1)
@@ -259,40 +259,44 @@
         return [side_by_side(pair) for pair in (evens, odds, odds_right, evens_left)]
 
     def lines_of(k, core):
-        pieces = []
-        for piece in range(z.pieces):
-            at = k * z.pieces + piece
-            pieces.append(sum(got_ref[source, core, at].astype(F32) for source in sources))
-        return stacked(pieces + blanks)
-
-    def split(value):
-        return [value[:, k : k + n] for k in range(0, value.shape[1], n)]
+        window = sum(got_ref[source, core, k].astype(F32) for source in sources)
+        return stacked([window[:, piece * n : (piece + 1) * n] for piece in range(z.pieces)] + blanks)
 
     def leading(base):
-        evens, odds = ([lines_of(base + k, core) for k in range(group)] for core in range(2))
-        field = stacked([stacked(blocks(evens, odds, lanes0)).astype(BF16), ones])
-        first = relu(nn_dot(k1_ref[...], field))
-        moves = blocks(split(first[: z.m1]), split(first[z.m1 :]), lanes1)[2:]
-        second = relu(nn_dot(k2_ref[...], stacked([first] + moves)))
-        reduced = relu(nn_dot(k3_ref[...], stacked([second, ones])))
-        for k, plane in enumerate(split(reduced)):
-            coarse[base + k + 1] = plane
+        fields = []
+        for k in range(0, group, 2):
+            evens, odds = ([lines_of(base + k, core), lines_of(base + k + 1, core)] for core in range(2))
+            fields.append(stacked([stacked(blocks(evens, odds, lanes0)).astype(BF16), ones]))
+        firsts = [relu(nn_dot(k1_ref[...], field)) for field in fields]
+        fields = []
+        for first in firsts:
+            even, odd = first[: z.m1], first[z.m1 :]
+            moves = blocks([even[:, :n], even[:, n:]], [odd[:, :n], odd[:, n:]], lanes1)[2:]
+            fields.append(stacked([first] + moves))
+        seconds = [relu(nn_dot(k2_ref[...], field)) for field in fields]
+        for k, second in enumerate(seconds):
+            reduced = relu(nn_dot(k3_ref[...], stacked([second, ones])))
+            coarse[base + 2 * k + 1] = reduced[:, :n]
+            coarse[base + 2 * k + 2] = reduced[:, n:]
 
     def trailing(base):
-        around = list(range(-1, group + 1)) if groups > 1 else list(range(group))
-        planes = [coarse[base + k + 1] for k in around]
-        field = stacked([
-            side_by_side([moved(plane, 1, lanes3) for plane in planes]),
-            side_by_side(planes),
-            side_by_side([moved(plane, -1, lanes3) for plane in planes]),
-            jnp.ones((TILE, len(planes) * n), BF16),
-        ])
-        terms = split(nn_dot(k4_ref[...], field))
+        planes = list(range(-1, group + 1)) if groups > 1 else list(range(group))
+        totals = [None] * group
+        for q in range(0, len(planes), 2):
+            pair = planes[q : q + 2]
+            fields = []
+            for k in pair:
+                plane = coarse[base + k + 1]
+                fields.append(stacked([moved(plane, 1, lanes3), plane, moved(plane, -1, lanes3), ones[:, :n]]))
+            terms = nn_dot(k4_ref[...], side_by_side(fields))
+            for side, k in enumerate(pair):
+                for i in range(3):
+                    to = k + 1 - i
+                    if 0 <= to < group:
+                        term = terms[i * z.m4 : (i + 1) * z.m4, side * n : (side + 1) * n]
+                        totals[to] = term if totals[to] is None else totals[to] + term
         for k in range(group):
-            parts = [
-                terms[around.index(k + i - 1)][i * z.m4 : (i + 1) * z.m4] for i in range(3) if k + i - 1 in around
-            ]
-            out_ref[base + k] = relu(sum(parts[1:], parts[0]))
+            out_ref[base + k] = relu(totals[k])
 
     if groups == 1:
         leading(0)
@@ -324,7 +328,7 @@
     )(volume)
     packed = pl.pallas_call(
         functools.partial(pack_kernel, z, chips, members),
-        out_shape=like((vols * members * slices * z.pieces, 4, z.half), BF16),
+        out_shape=like((vols * members * slices, 4, z.pieces * z.half), BF16),
         in_specs=[vmem] * 3,
         out_specs=vmem,
         compiler_params=pltpu.CompilerParams(vmem_limit_bytes=16 * 1024 * 1024),
@@ -335,7 +339,7 @@
         reduce_conv_weight, reduce_conv_bias, deep_weight, deep_offset,
     ))
     got = lax.all_to_all(packed, ("vol", "zs"), split_axis=0, concat_axis=0, tiled=True)
-    got = got.reshape(chips, 2, z.depth * z.pieces, 4, z.half)
+    got = got.reshape(chips, 2, z.depth, 4, z.pieces * z.half)
     prepared = pl.pallas_call(
         functools.partial(prepare_kernel, z, members),
         out_shape=(

time: 19.2 us -> 19.2 us (level)
  no operation moved by 1% of the time
where the time goes in v2:
time: 19.2 us; the launch traced here: 18.9 us
  starting transfers between devices  7.64 us (40%)
  waiting for transfers between devices  5.62 us (29%)
  Pallas kernels  3.86 us (20%)
  local copies, waits for them, and re-layouts  1.68 us (9%)
    all_to_all x1, starting transfers between devices, shards(): lax.all_to_all(packed, ('vol', 'zs'), split_axis=0, concat_axis=0, tiled=...  7.19 us
    all_to_all x1, waiting for transfers between devices, shards(): lax.all_to_all(packed, ('vol', 'zs'), split_axis=0, concat_axis=0, tiled=...  5.42 us
    pallas_call x1, Pallas kernels, shards(): pl.pallas_call(functools.partial(main_kernel, z, chips), out_shape=like((...  1.84 us
    unnamed x18, local copies, waits for them, and re-layouts  1.41 us
    pallas_call x1, Pallas kernels, shards(): pl.pallas_call(functools.partial(prepare_kernel, z, members), out_shape=(...  1.1 us
    pallas_call x1, Pallas kernels, shards(): pl.pallas_call(functools.partial(pack_kernel, z, chips, members), out_sha...  0.79 us
    ppermute x1, starting transfers between devices, shards(): other = lax.ppermute(volume, 'vol', [(v, v ^ 1) for v in range(vols)])  0.45 us
  transfers between devices with their start and end apart: 2, of which 2 were waited for; matrix products, arithmetic and copies ran while one was open for 1% of the time, Pallas kernels for 7%

profile of v2, /device:TPU:0, one launch (start us, length us, event | category | flops | bytes accessed | tf_op | source)
XLA Modules:
  0.0 18.9 jit_solution(16122595154144441645)
XLA Ops:
  0.0 0.5 %collective-permute-start = (bf16[1,32,256]{2,1,0:T(8,128)(2,1)}, bf16[1,32,256]{2,1,0:T(8,128)(2,1)S(1)}, u32[]{:S(2)}, u32[]{:S(2)}) collective-permute-start(bf16[1,32,256]{2,1,0:T(8,128)(2,1)} %own_ref.1), channel_id=1, source_target_pairs={{0,8},{8,0},{16,24},{24,16},{1,9},{9,1},{17,25},{25,17},{2,10},{10... | collective-permute-start | bytes 49160 | tf_op jit(solution)/shard_map/ppermute | solution.py:319
  0.5 0.0 copy-start.6
  0.5 0.7 %copy-done.6 = bf16[1,32,256]{2,1,0:T(8,128)(2,1)S(1)} copy-done((bf16[1,32,256]{2,1,0:T(8,128)(2,1)S(1)}, bf16[1,32,256]{2,1,0:T(8,128)(2,1)}, u32[]{:S(2)}) %copy-start.6) | copy-done | bytes 16408
  1.2 0.1 sort.1
  1.3 0.2 %collective-permute-done.other_ref = bf16[1,32,256]{2,1,0:T(8,128)(2,1)S(1)} collective-permute-done((bf16[1,32,256]{2,1,0:T(8,128)(2,1)}, bf16[1,32,256]{2,1,0:T(8,128)(2,1)S(1)}, u32[]{:S(2)}, u32[]{:S(2)}) %collective-permute-start) | collective-permute-done | bytes 16416 | tf_op jit(solution)/shard_map/ppermute | solution.py:319
  1.5 0.8 %pack.1 = bf16[32,4,384]{2,1,0:T(4,128)(2,1)} custom-call(f32[1,32,128]{2,1,0:T(8,128)S(1)} %get-tuple-element.20.own_ref, bf16[256,128]{1,0:T(8,128)(2,1)S(1)} %get-tuple-element.21.sort_ref, bf16[1,32,256]{2,1,0:T(8,128)(2,1)S(1)} %collective-permute-done.other_ref), custom_call_target="tpu_custom_call" | custom-call | tf_op jit(solution)/shard_map/pack/pallas_call | solution.py:329
  2.3 0.0 copy-start.8
  2.3 0.0 copy-start.7
  2.3 7.2 %all-to-all-start = ((bf16[32,4,384]{2,1,0:T(4,128)(2,1)}), bf16[32,4,384]{2,1,0:T(4,128)(2,1)S(1)}, u32[]{:S(2)}, u32[]{:S(2)}) async-start(bf16[32,4,384]{2,1,0:T(4,128)(2,1)} %pack.1), calls=%async_computation | async-start | bytes 196608 | tf_op jit(solution)/shard_map/all_to_all | solution.py:341
  9.5 0.0 copy-done.8
  9.5 0.0 copy-done.7
  9.5 0.0 copy-start
  9.5 0.0 copy-start.5
  9.6 0.3 %copy.11.w4_ref = bf16[27,24,24]{2,1,0:T(8,128)(2,1)S(1)} copy(bf16[27,24,24]{0,2,1:T(8,128)(2,1)S(1)} %copy-done.7) | data formatting | bytes 62208 | tf_op jit(solution)/shard_map/optimization_barrier | solution.py:337
  9.8 0.0 copy-start.1
  9.8 0.0 copy-start.2
  9.8 0.0 copy-start.3
  9.8 0.0 copy-start.4
  9.9 0.4 %copy-done = bf16[9,12,12]{2,1,0:T(8,128)(2,1)S(1)} copy-done((bf16[9,12,12]{2,1,0:T(8,128)(2,1)S(1)}, bf16[9,12,12]{2,1,0:T(8,128)(2,1)}, u32[]{:S(2)}) %copy-start) | copy-done | bytes 2616
  10.3 0.0 copy-done.5
  10.3 0.2 %copy-done.1 = bf16[9,12]{1,0:T(8,128)(2,1)S(1)} copy-done((bf16[9,12]{1,0:T(8,128)(2,1)S(1)}, bf16[9,12]{1,0:T(8,128)(2,1)}, u32[]{:S(2)}) %copy-start.1) | copy-done | bytes 240
  10.5 0.0 copy-done.2
  10.5 0.0 copy-done.3
  10.5 0.0 copy-done.4
  10.5 1.1 %prepare.1 = (bf16[256,80]{1,0:T(8,128)(2,1)S(1)}, bf16[192,512]{1,0:T(8,128)(2,1)S(1)}, bf16[96,208]{1,0:T(8,128)(2,1)S(1)}, bf16[144,304]{1,0:T(8,128)(2,1)S(1)}) custom-call(bf16[9,12]{1,0:T(8,128)(2,1)S(1)} %copy-done.1, f32[1,12]{1,0:T(1,128)S(1)} %bitcast.7, bf16[9,12,12]{2,1,0:T(8,128)(2,1)S(1)} %copy-done, f32[1,12]{1,0:T(1,128)S(1)} %bitcast.8, ...), custom_call_target="tpu_custom_call" | custom-call | flops 50000000 | bytes 1000000 | tf_op jit(solution)/shard_map/prepare/pallas_call | solution.py:343
  11.6 5.4 %all-to-all-done = bf16[32,4,384]{2,1,0:T(4,128)(2,1)S(1)} async-done(((bf16[32,4,384]{2,1,0:T(4,128)(2,1)}), bf16[32,4,384]{2,1,0:T(4,128)(2,1)S(1)}, u32[]{:S(2)}, u32[]{:S(2)}) %all-to-all-start) | async-done | bytes 98336 | tf_op jit(solution)/shard_map/all_to_all | solution.py:341
  17.1 1.8 %encode.1 = bf16[8,48,128]{2,1,0:T(8,128)(2,1)} custom-call(bf16[2,2,8,4,384]{4,3,2,1,0:T(4,128)(2,1)S(1)} %bitcast.6, bf16[256,80]{1,0:T(8,128)(2,1)S(1)} %get-tuple-element.31.k1_ref, bf16[192,512]{1,0:T(8,128)(2,1)S(1)} %get-tuple-element.32.k2_ref, bf16[96,208]{1,0:T(8,128)(2,1)S(1)} %get-tuple-element.33.k3_ref, ...), custom_call_target="tpu_custom_call" | custom-call | flops 2000000000 | bytes 2000000 | tf_op jit(solution)/shard_map/encode/pallas_call | solution.py:359
  (1 shorter events, 0.0 us)
Async XLA Ops:
  0.0 1.5 %collective-permute-start = (bf16[1,32,256]{2,1,0:T(8,128)(2,1)}, bf16[1,32,256]{2,1,0:T(8,128)(2,1)S(1)}, u32[]{:S(2)}, u32[]{:S(2)}) collective-permute-start(bf16[1,32,256]{2,1,0:T(8,128)(2,1)} %own_ref.1), channel_id=1, source_target_pairs={{0,8},{8,0},{16,24},{24,16},{1,9},{9,1},{17,25},{25,17},{2,10},{10... | collective-permute-start | bytes 49160 | tf_op jit(solution)/shard_map/ppermute | solution.py:319
  0.5 0.7 %copy-start.6 = (bf16[1,32,256]{2,1,0:T(8,128)(2,1)S(1)}, bf16[1,32,256]{2,1,0:T(8,128)(2,1)}, u32[]{:S(2)}) copy-start(bf16[1,32,256]{2,1,0:T(8,128)(2,1)} %own_ref.1) | copy-start | bytes 49156
  2.3 7.2 %copy-start.8 = (bf16[4,12,24]{2,0,1:T(4,128)(2,1)S(1)}, bf16[4,12,24]{2,0,1:T(4,128)(2,1)}, u32[]{:S(2)}) copy-start(bf16[4,12,24]{2,0,1:T(4,128)(2,1)} %param.14) | copy-start | bytes 6916
  2.3 7.2 %copy-start.7 = (bf16[27,24,24]{0,2,1:T(8,128)(2,1)S(1)}, bf16[27,24,24]{0,2,1:T(8,128)(2,1)}, u32[]{:S(2)}) copy-start(bf16[27,24,24]{0,2,1:T(8,128)(2,1)} %param.16) | copy-start | bytes 93316
  2.3 14.8 %all-to-all-start = ((bf16[32,4,384]{2,1,0:T(4,128)(2,1)}), bf16[32,4,384]{2,1,0:T(4,128)(2,1)S(1)}, u32[]{:S(2)}, u32[]{:S(2)}) async-start(bf16[32,4,384]{2,1,0:T(4,128)(2,1)} %pack.1), calls=%async_computation | async-start | bytes 196608 | tf_op jit(solution)/shard_map/all_to_all | solution.py:341
  9.5 0.8 %copy-start = (bf16[9,12,12]{2,1,0:T(8,128)(2,1)S(1)}, bf16[9,12,12]{2,1,0:T(8,128)(2,1)}, u32[]{:S(2)}) copy-start(bf16[9,12,12]{2,1,0:T(8,128)(2,1)} %w2_ref) | copy-start | bytes 7780
  9.5 0.8 %copy-start.5 = (f32[24]{0:T(128)S(1)}, f32[24]{0:T(128)}, u32[]{:S(2)}) copy-start(f32[24]{0:T(128)} %param.17) | copy-start | bytes 292
  9.8 0.7 %copy-start.1 = (bf16[9,12]{1,0:T(8,128)(2,1)S(1)}, bf16[9,12]{1,0:T(8,128)(2,1)}, u32[]{:S(2)}) copy-start(bf16[9,12]{1,0:T(8,128)(2,1)} %w1_ref) | copy-start | bytes 652
  9.8 0.7 %copy-start.2 = (f32[12]{0:T(128)S(1)}, f32[12]{0:T(128)}, u32[]{:S(2)}) copy-start(f32[12]{0:T(128)} %param.11) | copy-start | bytes 148
  9.8 0.7 %copy-start.3 = (f32[12]{0:T(128)S(1)}, f32[12]{0:T(128)}, u32[]{:S(2)}) copy-start(f32[12]{0:T(128)} %param.13) | copy-start | bytes 148
  9.8 0.7 %copy-start.4 = (f32[24]{0:T(128)S(1)}, f32[24]{0:T(128)}, u32[]{:S(2)}) copy-start(f32[24]{0:T(128)} %param.15) | copy-start | bytes 292

commit v3 on v2

--- a/solution.py
+++ b/solution.py
@@ -249,9 +249,6 @@
     lanes0 = iota((z.lines, n), 1)
     lanes1 = iota((z.m1, n), 1)
     lanes3 = iota((z.m3, n), 1)
-    if groups > 1:
-        coarse[0] = jnp.zeros((z.m3, n), BF16)
-        coarse[z.depth + 1] = jnp.zeros((z.m3, n), BF16)
 
     def blocks(evens, odds, lanes):
         odds_right = [moved(odd, 1, lanes) for odd in odds]
@@ -260,13 +257,14 @@
 
     def lines_of(k, core):
         window = sum(got_ref[source, core, k].astype(F32) for source in sources)
-        return stacked([window[:, piece * n : (piece + 1) * n] for piece in range(z.pieces)] + blanks)
+        lines = [window[:, piece * n : (piece + 1) * n] for piece in range(z.pieces)]
+        return stacked(lines + blanks).astype(BF16)
 
     def leading(base):
         fields = []
         for k in range(0, group, 2):
             evens, odds = ([lines_of(base + k, core), lines_of(base + k + 1, core)] for core in range(2))
-            fields.append(stacked([stacked(blocks(evens, odds, lanes0)).astype(BF16), ones]))
+            fields.append(stacked(blocks(evens, odds, lanes0) + [ones]))
         firsts = [relu(nn_dot(k1_ref[...], field)) for field in fields]
         fields = []
         for first in firsts:
@@ -274,19 +272,19 @@
             moves = blocks([even[:, :n], even[:, n:]], [odd[:, :n], odd[:, n:]], lanes1)[2:]
             fields.append(stacked([first] + moves))
         seconds = [relu(nn_dot(k2_ref[...], field)) for field in fields]
-        for k, second in enumerate(seconds):
+        planes = []
+        for second in seconds:
             reduced = relu(nn_dot(k3_ref[...], stacked([second, ones])))
-            coarse[base + 2 * k + 1] = reduced[:, :n]
-            coarse[base + 2 * k + 2] = reduced[:, n:]
-
-    def trailing(base):
-        planes = list(range(-1, group + 1)) if groups > 1 else list(range(group))
+            planes += [reduced[:, :n], reduced[:, n:]]
+        return planes
+
+    def trailing(base, planes, values):
         totals = [None] * group
         for q in range(0, len(planes), 2):
             pair = planes[q : q + 2]
             fields = []
             for k in pair:
-                plane = coarse[base + k + 1]
+                plane = values[k]
                 fields.append(stacked([moved(plane, 1, lanes3), plane, moved(plane, -1, lanes3), ones[:, :n]]))
             terms = nn_dot(k4_ref[...], side_by_side(fields))
             for side, k in enumerate(pair):
@@ -299,11 +297,21 @@
             out_ref[base + k] = relu(totals[k])
 
     if groups == 1:
-        leading(0)
-        trailing(0)
-    else:
-        pl.loop(0, groups)(lambda g: leading(g * group))
-        pl.loop(0, groups)(lambda g: trailing(g * group))
+        trailing(0, list(range(group)), leading(0))
+        return
+
+    coarse[0] = jnp.zeros((z.m3, n), BF16)
+    coarse[z.depth + 1] = jnp.zeros((z.m3, n), BF16)
+
+    @pl.loop(0, groups)
+    def _(g):
+        for k, plane in enumerate(leading(g * group)):
+            coarse[g * group + k + 1] = plane
+
+    @pl.loop(0, groups)
+    def _(g):
+        around = list(range(-1, group + 1))
+        trailing(g * group, around, {k: coarse[g * group + k + 1] for k in around})
 
 
 def shards(

time: 19.2 us -> 19.2 us (level)
  no operation moved by 1% of the time
where the time goes in v3:
time: 19.2 us; the launch traced here: 18.9 us
  starting transfers between devices  7.64 us (40%)
  waiting for transfers between devices  5.62 us (29%)
  Pallas kernels  3.83 us (20%)
  local copies, waits for them, and re-layouts  1.68 us (9%)
    all_to_all x1, starting transfers between devices, shards(): lax.all_to_all(packed, ('vol', 'zs'), split_axis=0, concat_axis=0, tiled=...  7.19 us
    all_to_all x1, waiting for transfers between devices, shards(): lax.all_to_all(packed, ('vol', 'zs'), split_axis=0, concat_axis=0, tiled=...  5.42 us
    pallas_call x1, Pallas kernels, shards(): pl.pallas_call(functools.partial(main_kernel, z, chips), out_shape=like((...  1.81 us
    unnamed x18, local copies, waits for them, and re-layouts  1.41 us
    pallas_call x1, Pallas kernels, shards(): pl.pallas_call(functools.partial(prepare_kernel, z, members), out_shape=(...  1.1 us
    pallas_call x1, Pallas kernels, shards(): pl.pallas_call(functools.partial(pack_kernel, z, chips, members), out_sha...  0.79 us
    ppermute x1, starting transfers between devices, shards(): other = lax.ppermute(volume, 'vol', [(v, v ^ 1) for v in range(vols)])  0.45 us
  transfers between devices with their start and end apart: 2, of which 2 were waited for; matrix products, arithmetic and copies ran while one was open for 1% of the time, Pallas kernels for 7%

profile of v3, /device:TPU:0, one launch (start us, length us, event | category | flops | bytes accessed | tf_op | source)
XLA Modules:
  0.0 18.9 jit_solution(10541765855251721104)
XLA Ops:
  0.0 0.5 %collective-permute-start = (bf16[1,32,256]{2,1,0:T(8,128)(2,1)}, bf16[1,32,256]{2,1,0:T(8,128)(2,1)S(1)}, u32[]{:S(2)}, u32[]{:S(2)}) collective-permute-start(bf16[1,32,256]{2,1,0:T(8,128)(2,1)} %own_ref.1), channel_id=1, source_target_pairs={{0,8},{8,0},{16,24},{24,16},{1,9},{9,1},{17,25},{25,17},{2,10},{10... | collective-permute-start | bytes 49160 | tf_op jit(solution)/shard_map/ppermute | solution.py:327
  0.5 0.0 copy-start.6
  0.5 0.7 %copy-done.6 = bf16[1,32,256]{2,1,0:T(8,128)(2,1)S(1)} copy-done((bf16[1,32,256]{2,1,0:T(8,128)(2,1)S(1)}, bf16[1,32,256]{2,1,0:T(8,128)(2,1)}, u32[]{:S(2)}) %copy-start.6) | copy-done | bytes 16408
  1.2 0.1 sort.1
  1.3 0.2 %collective-permute-done.other_ref = bf16[1,32,256]{2,1,0:T(8,128)(2,1)S(1)} collective-permute-done((bf16[1,32,256]{2,1,0:T(8,128)(2,1)}, bf16[1,32,256]{2,1,0:T(8,128)(2,1)S(1)}, u32[]{:S(2)}, u32[]{:S(2)}) %collective-permute-start) | collective-permute-done | bytes 16416 | tf_op jit(solution)/shard_map/ppermute | solution.py:327
  1.5 0.8 %pack.1 = bf16[32,4,384]{2,1,0:T(4,128)(2,1)} custom-call(f32[1,32,128]{2,1,0:T(8,128)S(1)} %get-tuple-element.20.own_ref, bf16[256,128]{1,0:T(8,128)(2,1)S(1)} %get-tuple-element.21.sort_ref, bf16[1,32,256]{2,1,0:T(8,128)(2,1)S(1)} %collective-permute-done.other_ref), custom_call_target="tpu_custom_call" | custom-call | tf_op jit(solution)/shard_map/pack/pallas_call | solution.py:337
  2.3 0.0 copy-start.8
  2.3 0.0 copy-start.7
  2.3 7.2 %all-to-all-start = ((bf16[32,4,384]{2,1,0:T(4,128)(2,1)}), bf16[32,4,384]{2,1,0:T(4,128)(2,1)S(1)}, u32[]{:S(2)}, u32[]{:S(2)}) async-start(bf16[32,4,384]{2,1,0:T(4,128)(2,1)} %pack.1), calls=%async_computation | async-start | bytes 196608 | tf_op jit(solution)/shard_map/all_to_all | solution.py:349
  9.5 0.0 copy-done.8
  9.5 0.0 copy-done.7
  9.5 0.0 copy-start
  9.5 0.0 copy-start.5
  9.6 0.3 %copy.11.w4_ref = bf16[27,24,24]{2,1,0:T(8,128)(2,1)S(1)} copy(bf16[27,24,24]{0,2,1:T(8,128)(2,1)S(1)} %copy-done.7) | data formatting | bytes 62208 | tf_op jit(solution)/shard_map/optimization_barrier | solution.py:345
  9.8 0.0 copy-start.1
  9.8 0.0 copy-start.2
  9.8 0.0 copy-start.3
  9.8 0.0 copy-start.4
  9.9 0.4 %copy-done = bf16[9,12,12]{2,1,0:T(8,128)(2,1)S(1)} copy-done((bf16[9,12,12]{2,1,0:T(8,128)(2,1)S(1)}, bf16[9,12,12]{2,1,0:T(8,128)(2,1)}, u32[]{:S(2)}) %copy-start) | copy-done | bytes 2616
  10.3 0.0 copy-done.5
  10.3 0.2 %copy-done.1 = bf16[9,12]{1,0:T(8,128)(2,1)S(1)} copy-done((bf16[9,12]{1,0:T(8,128)(2,1)S(1)}, bf16[9,12]{1,0:T(8,128)(2,1)}, u32[]{:S(2)}) %copy-start.1) | copy-done | bytes 240
  10.5 0.0 copy-done.2
  10.5 0.0 copy-done.3
  10.5 0.0 copy-done.4
  10.5 1.1 %prepare.1 = (bf16[256,80]{1,0:T(8,128)(2,1)S(1)}, bf16[192,512]{1,0:T(8,128)(2,1)S(1)}, bf16[96,208]{1,0:T(8,128)(2,1)S(1)}, bf16[144,304]{1,0:T(8,128)(2,1)S(1)}) custom-call(bf16[9,12]{1,0:T(8,128)(2,1)S(1)} %copy-done.1, f32[1,12]{1,0:T(1,128)S(1)} %bitcast.7, bf16[9,12,12]{2,1,0:T(8,128)(2,1)S(1)} %copy-done, f32[1,12]{1,0:T(1,128)S(1)} %bitcast.8, ...), custom_call_target="tpu_custom_call" | custom-call | flops 50000000 | bytes 1000000 | tf_op jit(solution)/shard_map/prepare/pallas_call | solution.py:351
  11.6 5.4 %all-to-all-done = bf16[32,4,384]{2,1,0:T(4,128)(2,1)S(1)} async-done(((bf16[32,4,384]{2,1,0:T(4,128)(2,1)}), bf16[32,4,384]{2,1,0:T(4,128)(2,1)S(1)}, u32[]{:S(2)}, u32[]{:S(2)}) %all-to-all-start) | async-done | bytes 98336 | tf_op jit(solution)/shard_map/all_to_all | solution.py:349
  17.1 1.8 %encode.1 = bf16[8,48,128]{2,1,0:T(8,128)(2,1)} custom-call(bf16[2,2,8,4,384]{4,3,2,1,0:T(4,128)(2,1)S(1)} %bitcast.6, bf16[256,80]{1,0:T(8,128)(2,1)S(1)} %get-tuple-element.31.k1_ref, bf16[192,512]{1,0:T(8,128)(2,1)S(1)} %get-tuple-element.32.k2_ref, bf16[96,208]{1,0:T(8,128)(2,1)S(1)} %get-tuple-element.33.k3_ref, ...), custom_call_target="tpu_custom_call" | custom-call | flops 2000000000 | bytes 2000000 | tf_op jit(solution)/shard_map/encode/pallas_call | solution.py:367
  (1 shorter events, 0.0 us)
Async XLA Ops:
  0.0 1.5 %collective-permute-start = (bf16[1,32,256]{2,1,0:T(8,128)(2,1)}, bf16[1,32,256]{2,1,0:T(8,128)(2,1)S(1)}, u32[]{:S(2)}, u32[]{:S(2)}) collective-permute-start(bf16[1,32,256]{2,1,0:T(8,128)(2,1)} %own_ref.1), channel_id=1, source_target_pairs={{0,8},{8,0},{16,24},{24,16},{1,9},{9,1},{17,25},{25,17},{2,10},{10... | collective-permute-start | bytes 49160 | tf_op jit(solution)/shard_map/ppermute | solution.py:327
  0.5 0.7 %copy-start.6 = (bf16[1,32,256]{2,1,0:T(8,128)(2,1)S(1)}, bf16[1,32,256]{2,1,0:T(8,128)(2,1)}, u32[]{:S(2)}) copy-start(bf16[1,32,256]{2,1,0:T(8,128)(2,1)} %own_ref.1) | copy-start | bytes 49156
  2.3 7.2 %copy-start.8 = (bf16[4,12,24]{2,0,1:T(4,128)(2,1)S(1)}, bf16[4,12,24]{2,0,1:T(4,128)(2,1)}, u32[]{:S(2)}) copy-start(bf16[4,12,24]{2,0,1:T(4,128)(2,1)} %param.14) | copy-start | bytes 6916
  2.3 7.2 %copy-start.7 = (bf16[27,24,24]{0,2,1:T(8,128)(2,1)S(1)}, bf16[27,24,24]{0,2,1:T(8,128)(2,1)}, u32[]{:S(2)}) copy-start(bf16[27,24,24]{0,2,1:T(8,128)(2,1)} %param.16) | copy-start | bytes 93316
  2.3 14.8 %all-to-all-start = ((bf16[32,4,384]{2,1,0:T(4,128)(2,1)}), bf16[32,4,384]{2,1,0:T(4,128)(2,1)S(1)}, u32[]{:S(2)}, u32[]{:S(2)}) async-start(bf16[32,4,384]{2,1,0:T(4,128)(2,1)} %pack.1), calls=%async_computation | async-start | bytes 196608 | tf_op jit(solution)/shard_map/all_to_all | solution.py:349
  9.5 0.8 %copy-start = (bf16[9,12,12]{2,1,0:T(8,128)(2,1)S(1)}, bf16[9,12,12]{2,1,0:T(8,128)(2,1)}, u32[]{:S(2)}) copy-start(bf16[9,12,12]{2,1,0:T(8,128)(2,1)} %w2_ref) | copy-start | bytes 7780
  9.5 0.8 %copy-start.5 = (f32[24]{0:T(128)S(1)}, f32[24]{0:T(128)}, u32[]{:S(2)}) copy-start(f32[24]{0:T(128)} %param.17) | copy-start | bytes 292
  9.8 0.7 %copy-start.1 = (bf16[9,12]{1,0:T(8,128)(2,1)S(1)}, bf16[9,12]{1,0:T(8,128)(2,1)}, u32[]{:S(2)}) copy-start(bf16[9,12]{1,0:T(8,128)(2,1)} %w1_ref) | copy-start | bytes 652
  9.8 0.7 %copy-start.2 = (f32[12]{0:T(128)S(1)}, f32[12]{0:T(128)}, u32[]{:S(2)}) copy-start(f32[12]{0:T(128)} %param.11) | copy-start | bytes 148
  9.8 0.7 %copy-start.3 = (f32[12]{0:T(128)S(1)}, f32[12]{0:T(128)}, u32[]{:S(2)}) copy-start(f32[12]{0:T(128)} %param.13) | copy-start | bytes 148
  9.8 0.7 %copy-start.4 = (f32[24]{0:T(128)S(1)}, f32[24]{0:T(128)}, u32[]{:S(2)}) copy-start(f32[24]{0:T(128)} %param.15) | copy-start | bytes 292

commit v4 on v2

--- a/solution.py
+++ b/solution.py
@@ -65,16 +65,17 @@
         return 2 * self.strip * member - 4
 
 
-def sort_kernel(z, own_ref, sort_ref, sorted_ref):
-    core = lax.rem(lax.axis_index("vol"), 2)
-    shape = (z.cols, z.half)
-    sort = one_hot(iota(shape, 0) == 2 * iota(shape, 1) + core)
-    sort_ref[...] = sort
-    for s in range(own_ref.shape[0]):
-        sorted_ref[s] = nn_dot(own_ref[s], sort)
-
-
-def pack_kernel(z, chips, members, own_ref, sort_ref, other_ref, packed_ref):
+def half_of(lines, first_core, z):
+    return jnp.where(first_core, lines[:, : z.half], lines[:, z.half :])
+
+
+def load_kernel(z, volume_ref, own_ref):
+    first_core = lax.rem(lax.axis_index("vol"), 2) == 0
+    for s in range(volume_ref.shape[0]):
+        own_ref[s] = half_of(volume_ref[s].astype(F32), first_core, z)
+
+
+def pack_kernel(z, chips, members, own_ref, other_ref, packed_ref):
     vol = lax.axis_index("vol")
     chip = lax.div(vol, 2)
     first_core = vol - 2 * chip == 0
@@ -82,7 +83,7 @@
     slices = own_ref.shape[0]
     empty = jnp.zeros((4, z.half), BF16)
     for s in range(slices):
-        own, other = own_ref[s], nn_dot(other_ref[s], sort_ref[...])
+        own, other = own_ref[s], half_of(other_ref[s].astype(F32), first_core, z)
         lines = stacked([jnp.where(first_core, own, other), jnp.where(first_core, other, own)])
         pieces = [lines[row : row + 4].astype(BF16) for row in range(0, 2 * z.rows, 4)]
 
@@ -107,10 +108,16 @@
 
 def prepare_kernel(
     z, members, w1_ref, b1_ref, w2_ref, b2_ref, w3_ref, b3_ref, w4_ref, b4_ref,
-    k1_ref, k2_ref, k3_ref, k4_ref,
+    sort_ref, k1_ref, k2_ref, k3_ref, k4_ref,
 ):
     member = lax.axis_index("zs")
     start = (lax.axis_index("vol") * members + member) * (2 * z.strip)
+    shape = (z.cols, 4 * z.half)
+    col = iota(shape, 1)
+    block = div(col, z.half)
+    step = jnp.where(block == 0, 0, jnp.where(block == 1, 1, jnp.where(block == 2, -1, 2)))
+    sort_ref[...] = one_hot(iota(shape, 0) == 2 * (col - block * z.half) + step)
+
     def spread(rows, offsets, period, stretch):
         row = div(iota((rows, period), 0), stretch)
         at = row - div(row, period) * period
@@ -233,7 +240,7 @@
 
 
 def main_kernel(
-    z, chips, got_ref, k1_ref, k2_ref, k3_ref, k4_ref, out_ref, coarse,
+    z, chips, got_ref, sort_ref, k1_ref, k2_ref, k3_ref, k4_ref, out_ref, coarse,
 ):
     chip = lax.div(lax.axis_index("vol"), 2)
     sources = [chip]
@@ -246,7 +253,6 @@
     n = z.half
     ones = jnp.ones((TILE, z.cols), BF16)
     blanks = [jnp.zeros((z.lines - z.window, n), F32)] if z.lines > z.window else []
-    lanes0 = iota((z.lines, n), 1)
     lanes1 = iota((z.m1, n), 1)
     lanes3 = iota((z.m3, n), 1)
     if groups > 1:
@@ -260,13 +266,18 @@
 
     def lines_of(k, core):
         window = sum(got_ref[source, core, k].astype(F32) for source in sources)
-        return stacked([window[:, piece * n : (piece + 1) * n] for piece in range(z.pieces)] + blanks)
+        lines = [window[:, piece * n : (piece + 1) * n] for piece in range(z.pieces)]
+        return stacked(lines + blanks).astype(BF16)
 
     def leading(base):
+        lines = stacked([side_by_side([lines_of(base + k, core) for core in range(2)]) for k in range(group)])
+        lines = nn_dot(lines, sort_ref[...]).astype(BF16)
         fields = []
         for k in range(0, group, 2):
-            evens, odds = ([lines_of(base + k, core), lines_of(base + k + 1, core)] for core in range(2))
-            fields.append(stacked([stacked(blocks(evens, odds, lanes0)).astype(BF16), ones]))
+            pair = [lines[at * z.lines : (at + 1) * z.lines] for at in (k, k + 1)]
+            fields.append(
+                stacked([side_by_side([side[:, b : b + n] for side in pair]) for b in range(0, 4 * n, n)] + [ones])
+            )
         firsts = [relu(nn_dot(k1_ref[...], field)) for field in fields]
         fields = []
         for first in firsts:
@@ -317,23 +328,23 @@
     like = jax.ShapeDtypeStruct
     chips = vols // 2
     other = lax.ppermute(volume, "vol", [(v, v ^ 1) for v in range(vols)])
-    sort, own = pl.pallas_call(
-        functools.partial(sort_kernel, z),
-        out_shape=(like((z.cols, z.half), BF16), like((slices, z.rows, z.half), F32)),
+    own = pl.pallas_call(
+        functools.partial(load_kernel, z),
+        out_shape=like((slices, z.rows, z.half), F32),
         in_specs=[vmem],
-        out_specs=(vmem,) * 2,
+        out_specs=vmem,
         compiler_params=pltpu.CompilerParams(vmem_limit_bytes=16 * 1024 * 1024),
         cost_estimate=pl.CostEstimate(flops=5_000_000, bytes_accessed=100_000, transcendentals=0),
-        name="sort",
+        name="load",
     )(volume)
     packed = pl.pallas_call(
         functools.partial(pack_kernel, z, chips, members),
         out_shape=like((vols * members * slices, 4, z.pieces * z.half), BF16),
-        in_specs=[vmem] * 3,
+        in_specs=[vmem] * 2,
         out_specs=vmem,
         compiler_params=pltpu.CompilerParams(vmem_limit_bytes=16 * 1024 * 1024),
         name="pack",
-    )(own, sort, other)
+    )(own, other)
     packed, *parameters = lax.optimization_barrier((
         packed, first_weight, first_offset, second_weight, second_offset,
         reduce_conv_weight, reduce_conv_bias, deep_weight, deep_offset,
@@ -343,13 +354,14 @@
     prepared = pl.pallas_call(
         functools.partial(prepare_kernel, z, members),
         out_shape=(
+            like((z.cols, 4 * z.half), BF16),
             like((2 * z.m1, 4 * z.lines + TILE), BF16),
             like((2 * z.m2, 4 * z.m1), BF16),
             like((z.m3, 2 * z.m2 + TILE), BF16),
             like((3 * z.m4, 3 * z.m3 + TILE), BF16),
         ),
         in_specs=[vmem] * 8,
-        out_specs=(vmem,) * 4,
+        out_specs=(vmem,) * 5,
         compiler_params=pltpu.CompilerParams(vmem_limit_bytes=16 * 1024 * 1024),
         cost_estimate=pl.CostEstimate(flops=50_000_000, bytes_accessed=1_000_000, transcendentals=0),
         name="prepare",
@@ -359,7 +371,7 @@
     affinity = pl.pallas_call(
         functools.partial(main_kernel, z, chips),
         out_shape=like((z.depth, z.m4, z.half), BF16),
-        in_specs=[vmem] * 5,
+        in_specs=[vmem] * 6,
         out_specs=vmem,
         scratch_shapes=[
             pltpu.VMEM((z.depth + 2, z.m3, z.half), BF16),

time: 19.2 us -> 19.2 us (level)
  transfers between devices with their start and end apart: 2 -> 2, of which waited for: 2 -> 2; matrix products, arithmetic and copies ran while one was open for 1% -> 1% of each run, Pallas kernels for 7% -> 6%
where the time goes in v4:
time: 19.2 us; the launch traced here: 18.8 us
  starting transfers between devices  7.64 us (40%)
  waiting for transfers between devices  5.69 us (30%)
  Pallas kernels  3.75 us (20%)
  local copies, waits for them, and re-layouts  1.68 us (9%)
    all_to_all x1, starting transfers between devices, shards(): lax.all_to_all(packed, ('vol', 'zs'), split_axis=0, concat_axis=0, tiled=...  7.19 us
    all_to_all x1, waiting for transfers between devices, shards(): lax.all_to_all(packed, ('vol', 'zs'), split_axis=0, concat_axis=0, tiled=...  5.36 us
    pallas_call x1, Pallas kernels, shards(): pl.pallas_call(functools.partial(main_kernel, z, chips), out_shape=like((...  1.91 us
    unnamed x18, local copies, waits for them, and re-layouts  1.41 us
    pallas_call x1, Pallas kernels, shards(): pl.pallas_call(functools.partial(prepare_kernel, z, members), out_shape=(...  1.16 us
    pallas_call x1, Pallas kernels, shards(): pl.pallas_call(functools.partial(pack_kernel, z, chips, members), out_sha...  0.67 us
    ppermute x1, starting transfers between devices, shards(): other = lax.ppermute(volume, 'vol', [(v, v ^ 1) for v in range(vols)])  0.45 us
  transfers between devices with their start and end apart: 2, of which 2 were waited for; matrix products, arithmetic and copies ran while one was open for 1% of the time, Pallas kernels for 6%

profile of v4, /device:TPU:0, one launch (start us, length us, event | category | flops | bytes accessed | tf_op | source)
XLA Modules:
  0.0 18.8 jit_solution(15651183621038175068)
XLA Ops:
  0.0 0.5 %collective-permute-start = (bf16[1,32,256]{2,1,0:T(8,128)(2,1)}, bf16[1,32,256]{2,1,0:T(8,128)(2,1)S(1)}, u32[]{:S(2)}, u32[]{:S(2)}) collective-permute-start(bf16[1,32,256]{2,1,0:T(8,128)(2,1)} %volume_ref.1), channel_id=1, source_target_pairs={{0,8},{8,0},{16,24},{24,16},{1,9},{9,1},{17,25},{25,17},{2,10},{10... | collective-permute-start | bytes 49160 | tf_op jit(solution)/shard_map/ppermute | solution.py:330
  0.5 0.0 copy-start.1
  0.5 0.7 %copy-done.1 = bf16[1,32,256]{2,1,0:T(8,128)(2,1)S(1)} copy-done((bf16[1,32,256]{2,1,0:T(8,128)(2,1)S(1)}, bf16[1,32,256]{2,1,0:T(8,128)(2,1)}, u32[]{:S(2)}) %copy-start.1) | copy-done | bytes 16408
  1.2 0.0 copy-start.7
  1.2 0.3 %collective-permute-done.other_ref = bf16[1,32,256]{2,1,0:T(8,128)(2,1)S(1)} collective-permute-done((bf16[1,32,256]{2,1,0:T(8,128)(2,1)}, bf16[1,32,256]{2,1,0:T(8,128)(2,1)S(1)}, u32[]{:S(2)}, u32[]{:S(2)}) %collective-permute-start) | collective-permute-done | bytes 16416 | tf_op jit(solution)/shard_map/ppermute | solution.py:330
  1.5 0.7 %pack.1 = bf16[32,4,384]{2,1,0:T(4,128)(2,1)} custom-call(f32[1,32,128]{2,1,0:T(8,128)S(1)} %load.1.own_ref, bf16[1,32,256]{2,1,0:T(8,128)(2,1)S(1)} %collective-permute-done.other_ref), custom_call_target="tpu_custom_call" | custom-call | tf_op jit(solution)/shard_map/pack/pallas_call | solution.py:340
  2.2 0.0 copy-start.8
  2.2 7.2 %all-to-all-start = ((bf16[32,4,384]{2,1,0:T(4,128)(2,1)}), bf16[32,4,384]{2,1,0:T(4,128)(2,1)S(1)}, u32[]{:S(2)}, u32[]{:S(2)}) async-start(bf16[32,4,384]{2,1,0:T(4,128)(2,1)} %pack.1), calls=%async_computation | async-start | bytes 196608 | tf_op jit(solution)/shard_map/all_to_all | solution.py:352
  9.4 0.0 copy-done.8
  9.4 0.0 copy-done.7
  9.4 0.0 copy-start
  9.4 0.0 copy-start.6
  9.4 0.3 %copy.11.w4_ref = bf16[27,24,24]{2,1,0:T(8,128)(2,1)S(1)} copy(bf16[27,24,24]{0,2,1:T(8,128)(2,1)S(1)} %copy-done.7) | data formatting | bytes 62208 | tf_op jit(solution)/shard_map/optimization_barrier | solution.py:348
  9.7 0.0 copy-start.2
  9.7 0.0 copy-start.3
  9.7 0.0 copy-start.4
  9.7 0.0 copy-start.5
  9.7 0.4 %copy-done = bf16[9,12,12]{2,1,0:T(8,128)(2,1)S(1)} copy-done((bf16[9,12,12]{2,1,0:T(8,128)(2,1)S(1)}, bf16[9,12,12]{2,1,0:T(8,128)(2,1)}, u32[]{:S(2)}) %copy-start) | copy-done | bytes 2616
  10.2 0.0 copy-done.6
  10.2 0.2 %copy-done.2 = bf16[9,12]{1,0:T(8,128)(2,1)S(1)} copy-done((bf16[9,12]{1,0:T(8,128)(2,1)S(1)}, bf16[9,12]{1,0:T(8,128)(2,1)}, u32[]{:S(2)}) %copy-start.2) | copy-done | bytes 240
  10.4 0.0 copy-done.3
  10.4 0.0 copy-done.4
  10.4 0.0 copy-done.5
  10.4 1.2 %prepare.1 = (bf16[256,512]{1,0:T(8,128)(2,1)S(1)}, bf16[256,80]{1,0:T(8,128)(2,1)S(1)}, bf16[192,512]{1,0:T(8,128)(2,1)S(1)}, bf16[96,208]{1,0:T(8,128)(2,1)S(1)}, bf16[144,304]{1,0:T(8,128)(2,1)S(1)}) custom-call(bf16[9,12]{1,0:T(8,128)(2,1)S(1)} %copy-done.2, f32[1,12]{1,0:T(1,128)S(1)} %bitcast.7, bf16[9,12,12]{2,1,0:T(8,128)(2,1)S(1)} %copy-done, ...), custom_call_target="tpu_custom_call" | custom-call | flops 50000000 | bytes 1000000 | tf_op jit(solution)/shard_map/prepare/pallas_call | solution.py:354
  11.6 5.4 %all-to-all-done = bf16[32,4,384]{2,1,0:T(4,128)(2,1)S(1)} async-done(((bf16[32,4,384]{2,1,0:T(4,128)(2,1)}), bf16[32,4,384]{2,1,0:T(4,128)(2,1)S(1)}, u32[]{:S(2)}, u32[]{:S(2)}) %all-to-all-start) | async-done | bytes 98336 | tf_op jit(solution)/shard_map/all_to_all | solution.py:352
  16.9 1.9 %encode.1 = bf16[8,48,128]{2,1,0:T(8,128)(2,1)} custom-call(bf16[2,2,8,4,384]{4,3,2,1,0:T(4,128)(2,1)S(1)} %bitcast.6, bf16[256,512]{1,0:T(8,128)(2,1)S(1)} %get-tuple-element.28.sort_ref, bf16[256,80]{1,0:T(8,128)(2,1)S(1)} %get-tuple-element.29.k1_ref, bf16[192,512]{1,0:T(8,128)(2,1)S(1)} %get-tuple-element.30.k2_ref, ...), custom_call_target="tpu_custom_call" | custom-call | flops 2000000000 | bytes 2000000 | tf_op jit(solution)/shard_map/encode/pallas_call | solution.py:371
  (2 shorter events, 0.0 us)
Async XLA Ops:
  0.0 1.5 %collective-permute-start = (bf16[1,32,256]{2,1,0:T(8,128)(2,1)}, bf16[1,32,256]{2,1,0:T(8,128)(2,1)S(1)}, u32[]{:S(2)}, u32[]{:S(2)}) collective-permute-start(bf16[1,32,256]{2,1,0:T(8,128)(2,1)} %volume_ref.1), channel_id=1, source_target_pairs={{0,8},{8,0},{16,24},{24,16},{1,9},{9,1},{17,25},{25,17},{2,10},{10... | collective-permute-start | bytes 49160 | tf_op jit(solution)/shard_map/ppermute | solution.py:330
  0.5 0.7 %copy-start.1 = (bf16[1,32,256]{2,1,0:T(8,128)(2,1)S(1)}, bf16[1,32,256]{2,1,0:T(8,128)(2,1)}, u32[]{:S(2)}) copy-start(bf16[1,32,256]{2,1,0:T(8,128)(2,1)} %volume_ref.1) | copy-start | bytes 49156
  1.2 8.2 %copy-start.7 = (bf16[27,24,24]{0,2,1:T(8,128)(2,1)S(1)}, bf16[27,24,24]{0,2,1:T(8,128)(2,1)}, u32[]{:S(2)}) copy-start(bf16[27,24,24]{0,2,1:T(8,128)(2,1)} %param.16) | copy-start | bytes 93316
  2.2 7.2 %copy-start.8 = (bf16[4,12,24]{2,0,1:T(4,128)(2,1)S(1)}, bf16[4,12,24]{2,0,1:T(4,128)(2,1)}, u32[]{:S(2)}) copy-start(bf16[4,12,24]{2,0,1:T(4,128)(2,1)} %param.14) | copy-start | bytes 6916
  2.2 14.8 %all-to-all-start = ((bf16[32,4,384]{2,1,0:T(4,128)(2,1)}), bf16[32,4,384]{2,1,0:T(4,128)(2,1)S(1)}, u32[]{:S(2)}, u32[]{:S(2)}) async-start(bf16[32,4,384]{2,1,0:T(4,128)(2,1)} %pack.1), calls=%async_computation | async-start | bytes 196608 | tf_op jit(solution)/shard_map/all_to_all | solution.py:352
  9.4 0.8 %copy-start = (bf16[9,12,12]{2,1,0:T(8,128)(2,1)S(1)}, bf16[9,12,12]{2,1,0:T(8,128)(2,1)}, u32[]{:S(2)}) copy-start(bf16[9,12,12]{2,1,0:T(8,128)(2,1)} %w2_ref) | copy-start | bytes 7780
  9.4 0.8 %copy-start.6 = (f32[24]{0:T(128)S(1)}, f32[24]{0:T(128)}, u32[]{:S(2)}) copy-start(f32[24]{0:T(128)} %param.17) | copy-start | bytes 292
  9.7 0.7 %copy-start.2 = (bf16[9,12]{1,0:T(8,128)(2,1)S(1)}, bf16[9,12]{1,0:T(8,128)(2,1)}, u32[]{:S(2)}) copy-start(bf16[9,12]{1,0:T(8,128)(2,1)} %w1_ref) | copy-start | bytes 652
  9.7 0.7 %copy-start.3 = (f32[12]{0:T(128)S(1)}, f32[12]{0:T(128)}, u32[]{:S(2)}) copy-start(f32[12]{0:T(128)} %param.11) | copy-start | bytes 148
  9.7 0.7 %copy-start.4 = (f32[12]{0:T(128)S(1)}, f32[12]{0:T(128)}, u32[]{:S(2)}) copy-start(f32[12]{0:T(128)} %param.13) | copy-start | bytes 148
  9.7 0.7 %copy-start.5 = (f32[24]{0:T(128)S(1)}, f32[24]{0:T(128)}, u32[]{:S(2)}) copy-start(f32[24]{0:T(128)} %param.15) | copy-start | bytes 292

commit v5 on v2

--- a/solution.py
+++ b/solution.py
@@ -90,7 +90,7 @@
             for piece in range(z.pieces):
                 at = first // 4 + piece
                 value = pieces[at] if 0 <= at < len(pieces) else empty
-                packed_ref[to * slices + s, :, piece * z.half : (piece + 1) * z.half] = value
+                packed_ref[(to * slices + s) * z.pieces + piece] = value
 
         for core in range(2):
             for member in range(members):
@@ -233,7 +233,7 @@
 
 
 def main_kernel(
-    z, chips, got_ref, k1_ref, k2_ref, k3_ref, k4_ref, out_ref, coarse,
+    z, chips, got_ref, k1_ref, k2_ref, k3_ref, k4_ref, out_ref, coarse, result, sems,
 ):
     chip = lax.div(lax.axis_index("vol"), 2)
     sources = [chip]
@@ -259,8 +259,11 @@
         return [side_by_side(pair) for pair in (evens, odds, odds_right, evens_left)]
 
     def lines_of(k, core):
-        window = sum(got_ref[source, core, k].astype(F32) for source in sources)
-        return stacked([window[:, piece * n : (piece + 1) * n] for piece in range(z.pieces)] + blanks)
+        pieces = []
+        for piece in range(z.pieces):
+            at = k * z.pieces + piece
+            pieces.append(sum(got_ref[source, core, at].astype(F32) for source in sources))
+        return stacked(pieces + blanks)
 
     def leading(base):
         fields = []
@@ -281,7 +284,13 @@
 
     def trailing(base):
         planes = list(range(-1, group + 1)) if groups > 1 else list(range(group))
-        totals = [None] * group
+        totals = {}
+        half = max(group // 2, 1)
+        copies = [
+            pltpu.make_async_copy(result.at[pl.ds(at, half)], out_ref.at[pl.ds(base + at, half)], sems.at[number])
+            for number, at in enumerate(range(0, group, half))
+        ]
+        written = 0
         for q in range(0, len(planes), 2):
             pair = planes[q : q + 2]
             fields = []
@@ -292,11 +301,16 @@
             for side, k in enumerate(pair):
                 for i in range(3):
                     to = k + 1 - i
-                    if 0 <= to < group:
-                        term = terms[i * z.m4 : (i + 1) * z.m4, side * n : (side + 1) * n]
-                        totals[to] = term if totals[to] is None else totals[to] + term
-        for k in range(group):
-            out_ref[base + k] = relu(totals[k])
+                    term = terms[i * z.m4 : (i + 1) * z.m4, side * n : (side + 1) * n]
+                    totals[to] = totals[to] + term if to in totals else term
+            done = group if pair[-1] == planes[-1] else pair[-1]
+            while written < done:
+                result[written] = relu(totals[written])
+                written += 1
+                if written % half == 0:
+                    copies[written // half - 1].start()
+        for copy in copies:
+            copy.wait()
 
     if groups == 1:
         leading(0)
@@ -328,7 +342,7 @@
     )(volume)
     packed = pl.pallas_call(
         functools.partial(pack_kernel, z, chips, members),
-        out_shape=like((vols * members * slices, 4, z.pieces * z.half), BF16),
+        out_shape=like((vols * members * slices * z.pieces, 4, z.half), BF16),
         in_specs=[vmem] * 3,
         out_specs=vmem,
         compiler_params=pltpu.CompilerParams(vmem_limit_bytes=16 * 1024 * 1024),
@@ -339,7 +353,7 @@
         reduce_conv_weight, reduce_conv_bias, deep_weight, deep_offset,
     ))
     got = lax.all_to_all(packed, ("vol", "zs"), split_axis=0, concat_axis=0, tiled=True)
-    got = got.reshape(chips, 2, z.depth, 4, z.pieces * z.half)
+    got = got.reshape(chips, 2, z.depth * z.pieces, 4, z.half)
     prepared = pl.pallas_call(
         functools.partial(prepare_kernel, z, members),
         out_shape=(
@@ -360,9 +374,11 @@
         functools.partial(main_kernel, z, chips),
         out_shape=like((z.depth, z.m4, z.half), BF16),
         in_specs=[vmem] * 5,
-        out_specs=vmem,
+        out_specs=pl.BlockSpec(memory_space=pl.ANY),
         scratch_shapes=[
             pltpu.VMEM((z.depth + 2, z.m3, z.half), BF16),
+            pltpu.VMEM((min(z.depth, 8), z.m4, z.half), BF16),
+            pltpu.SemaphoreType.DMA((2,)),
         ],
         compiler_params=pltpu.CompilerParams(vmem_limit_bytes=32 * 1024 * 1024),
         cost_estimate=pl.CostEstimate(flops=2_000_000_000, bytes_accessed=2_000_000, transcendentals=0),

time: 19.2 us -> 19.2 us (level)
  no operation moved by 1% of the time
where the time goes in v5:
time: 19.2 us; the launch traced here: 18.9 us
  starting transfers between devices  7.64 us (40%)
  waiting for transfers between devices  5.62 us (29%)
  Pallas kernels  3.86 us (20%)
  local copies, waits for them, and re-layouts  1.68 us (9%)
    all_to_all x1, starting transfers between devices, shards(): lax.all_to_all(packed, ('vol', 'zs'), split_axis=0, concat_axis=0, tiled=...  7.19 us
    all_to_all x1, waiting for transfers between devices, shards(): lax.all_to_all(packed, ('vol', 'zs'), split_axis=0, concat_axis=0, tiled=...  5.42 us
    pallas_call x1, Pallas kernels, shards(): pl.pallas_call(functools.partial(main_kernel, z, chips), out_shape=like((...  1.84 us
    unnamed x18, local copies, waits for them, and re-layouts  1.41 us
    pallas_call x1, Pallas kernels, shards(): pl.pallas_call(functools.partial(prepare_kernel, z, members), out_shape=(...  1.1 us
    pallas_call x1, Pallas kernels, shards(): pl.pallas_call(functools.partial(pack_kernel, z, chips, members), out_sha...  0.79 us
    ppermute x1, starting transfers between devices, shards(): other = lax.ppermute(volume, 'vol', [(v, v ^ 1) for v in range(vols)])  0.45 us
  transfers between devices with their start and end apart: 2, of which 2 were waited for; matrix products, arithmetic and copies ran while one was open for 1% of the time, Pallas kernels for 7%

profile of v5, /device:TPU:0, one launch (start us, length us, event | category | flops | bytes accessed | tf_op | source)
XLA Modules:
  0.0 18.9 jit_solution(10878928637262660877)
XLA Ops:
  0.0 0.5 %collective-permute-start = (bf16[1,32,256]{2,1,0:T(8,128)(2,1)}, bf16[1,32,256]{2,1,0:T(8,128)(2,1)S(1)}, u32[]{:S(2)}, u32[]{:S(2)}) collective-permute-start(bf16[1,32,256]{2,1,0:T(8,128)(2,1)} %own_ref.1), channel_id=1, source_target_pairs={{0,8},{8,0},{16,24},{24,16},{1,9},{9,1},{17,25},{25,17},{2,10},{10... | collective-permute-start | bytes 49160 | tf_op jit(solution)/shard_map/ppermute | solution.py:333
  0.5 0.0 copy-start.6
  0.5 0.7 %copy-done.6 = bf16[1,32,256]{2,1,0:T(8,128)(2,1)S(1)} copy-done((bf16[1,32,256]{2,1,0:T(8,128)(2,1)S(1)}, bf16[1,32,256]{2,1,0:T(8,128)(2,1)}, u32[]{:S(2)}) %copy-start.6) | copy-done | bytes 16408
  1.2 0.1 sort.1
  1.3 0.2 %collective-permute-done.other_ref = bf16[1,32,256]{2,1,0:T(8,128)(2,1)S(1)} collective-permute-done((bf16[1,32,256]{2,1,0:T(8,128)(2,1)}, bf16[1,32,256]{2,1,0:T(8,128)(2,1)S(1)}, u32[]{:S(2)}, u32[]{:S(2)}) %collective-permute-start) | collective-permute-done | bytes 16416 | tf_op jit(solution)/shard_map/ppermute | solution.py:333
  1.5 0.8 %pack.1 = bf16[96,4,128]{2,1,0:T(4,128)(2,1)} custom-call(f32[1,32,128]{2,1,0:T(8,128)S(1)} %get-tuple-element.20.own_ref, bf16[256,128]{1,0:T(8,128)(2,1)S(1)} %get-tuple-element.21.sort_ref, bf16[1,32,256]{2,1,0:T(8,128)(2,1)S(1)} %collective-permute-done.other_ref), custom_call_target="tpu_custom_call" | custom-call | tf_op jit(solution)/shard_map/pack/pallas_call | solution.py:343
  2.3 0.0 copy-start.8
  2.3 0.0 copy-start.7
  2.3 7.2 %all-to-all-start = ((bf16[96,4,128]{2,1,0:T(4,128)(2,1)}), bf16[96,4,128]{2,1,0:T(4,128)(2,1)S(1)}, u32[]{:S(2)}, u32[]{:S(2)}) async-start(bf16[96,4,128]{2,1,0:T(4,128)(2,1)} %pack.1), calls=%async_computation | async-start | bytes 196608 | tf_op jit(solution)/shard_map/all_to_all | solution.py:355
  9.5 0.0 copy-done.8
  9.5 0.0 copy-done.7
  9.5 0.0 copy-start
  9.5 0.0 copy-start.5
  9.6 0.3 %copy.11.w4_ref = bf16[27,24,24]{2,1,0:T(8,128)(2,1)S(1)} copy(bf16[27,24,24]{0,2,1:T(8,128)(2,1)S(1)} %copy-done.7) | data formatting | bytes 62208 | tf_op jit(solution)/shard_map/optimization_barrier | solution.py:351
  9.8 0.0 copy-start.1
  9.8 0.0 copy-start.2
  9.8 0.0 copy-start.3
  9.8 0.0 copy-start.4
  9.9 0.4 %copy-done = bf16[9,12,12]{2,1,0:T(8,128)(2,1)S(1)} copy-done((bf16[9,12,12]{2,1,0:T(8,128)(2,1)S(1)}, bf16[9,12,12]{2,1,0:T(8,128)(2,1)}, u32[]{:S(2)}) %copy-start) | copy-done | bytes 2616
  10.3 0.0 copy-done.5
  10.3 0.2 %copy-done.1 = bf16[9,12]{1,0:T(8,128)(2,1)S(1)} copy-done((bf16[9,12]{1,0:T(8,128)(2,1)S(1)}, bf16[9,12]{1,0:T(8,128)(2,1)}, u32[]{:S(2)}) %copy-start.1) | copy-done | bytes 240
  10.5 0.0 copy-done.2
  10.5 0.0 copy-done.3
  10.5 0.0 copy-done.4
  10.5 1.1 %prepare.1 = (bf16[256,80]{1,0:T(8,128)(2,1)S(1)}, bf16[192,512]{1,0:T(8,128)(2,1)S(1)}, bf16[96,208]{1,0:T(8,128)(2,1)S(1)}, bf16[144,304]{1,0:T(8,128)(2,1)S(1)}) custom-call(bf16[9,12]{1,0:T(8,128)(2,1)S(1)} %copy-done.1, f32[1,12]{1,0:T(1,128)S(1)} %bitcast.7, bf16[9,12,12]{2,1,0:T(8,128)(2,1)S(1)} %copy-done, f32[1,12]{1,0:T(1,128)S(1)} %bitcast.8, ...), custom_call_target="tpu_custom_call" | custom-call | flops 50000000 | bytes 1000000 | tf_op jit(solution)/shard_map/prepare/pallas_call | solution.py:357
  11.6 5.4 %all-to-all-done = bf16[96,4,128]{2,1,0:T(4,128)(2,1)S(1)} async-done(((bf16[96,4,128]{2,1,0:T(4,128)(2,1)}), bf16[96,4,128]{2,1,0:T(4,128)(2,1)S(1)}, u32[]{:S(2)}, u32[]{:S(2)}) %all-to-all-start) | async-done | bytes 98336 | tf_op jit(solution)/shard_map/all_to_all | solution.py:355
  17.1 1.8 %encode.1 = bf16[8,48,128]{2,1,0:T(8,128)(2,1)} custom-call(bf16[2,2,24,4,128]{4,3,2,1,0:T(4,128)(2,1)S(1)} %bitcast.6, bf16[256,80]{1,0:T(8,128)(2,1)S(1)} %get-tuple-element.31.k1_ref, bf16[192,512]{1,0:T(8,128)(2,1)S(1)} %get-tuple-element.32.k2_ref, bf16[96,208]{1,0:T(8,128)(2,1)S(1)} %get-tuple-element.33.k3_ref, ...), custom_call_target="tpu_custom_call" | custom-call | flops 2000000000 | bytes 2000000 | tf_op jit(solution)/shard_map/encode/pallas_call | solution.py:373
  (1 shorter events, 0.0 us)
Async XLA Ops:
  0.0 1.5 %collective-permute-start = (bf16[1,32,256]{2,1,0:T(8,128)(2,1)}, bf16[1,32,256]{2,1,0:T(8,128)(2,1)S(1)}, u32[]{:S(2)}, u32[]{:S(2)}) collective-permute-start(bf16[1,32,256]{2,1,0:T(8,128)(2,1)} %own_ref.1), channel_id=1, source_target_pairs={{0,8},{8,0},{16,24},{24,16},{1,9},{9,1},{17,25},{25,17},{2,10},{10... | collective-permute-start | bytes 49160 | tf_op jit(solution)/shard_map/ppermute | solution.py:333
  0.5 0.7 %copy-start.6 = (bf16[1,32,256]{2,1,0:T(8,128)(2,1)S(1)}, bf16[1,32,256]{2,1,0:T(8,128)(2,1)}, u32[]{:S(2)}) copy-start(bf16[1,32,256]{2,1,0:T(8,128)(2,1)} %own_ref.1) | copy-start | bytes 49156
  2.3 7.2 %copy-start.8 = (bf16[4,12,24]{2,0,1:T(4,128)(2,1)S(1)}, bf16[4,12,24]{2,0,1:T(4,128)(2,1)}, u32[]{:S(2)}) copy-start(bf16[4,12,24]{2,0,1:T(4,128)(2,1)} %param.14) | copy-start | bytes 6916
  2.3 7.2 %copy-start.7 = (bf16[27,24,24]{0,2,1:T(8,128)(2,1)S(1)}, bf16[27,24,24]{0,2,1:T(8,128)(2,1)}, u32[]{:S(2)}) copy-start(bf16[27,24,24]{0,2,1:T(8,128)(2,1)} %param.16) | copy-start | bytes 93316
  2.3 14.8 %all-to-all-start = ((bf16[96,4,128]{2,1,0:T(4,128)(2,1)}), bf16[96,4,128]{2,1,0:T(4,128)(2,1)S(1)}, u32[]{:S(2)}, u32[]{:S(2)}) async-start(bf16[96,4,128]{2,1,0:T(4,128)(2,1)} %pack.1), calls=%async_computation | async-start | bytes 196608 | tf_op jit(solution)/shard_map/all_to_all | solution.py:355
  9.5 0.8 %copy-start = (bf16[9,12,12]{2,1,0:T(8,128)(2,1)S(1)}, bf16[9,12,12]{2,1,0:T(8,128)(2,1)}, u32[]{:S(2)}) copy-start(bf16[9,12,12]{2,1,0:T(8,128)(2,1)} %w2_ref) | copy-start | bytes 7780
  9.5 0.8 %copy-start.5 = (f32[24]{0:T(128)S(1)}, f32[24]{0:T(128)}, u32[]{:S(2)}) copy-start(f32[24]{0:T(128)} %param.17) | copy-start | bytes 292
  9.8 0.7 %copy-start.1 = (bf16[9,12]{1,0:T(8,128)(2,1)S(1)}, bf16[9,12]{1,0:T(8,128)(2,1)}, u32[]{:S(2)}) copy-start(bf16[9,12]{1,0:T(8,128)(2,1)} %w1_ref) | copy-start | bytes 652
  9.8 0.7 %copy-start.2 = (f32[12]{0:T(128)S(1)}, f32[12]{0:T(128)}, u32[]{:S(2)}) copy-start(f32[12]{0:T(128)} %param.11) | copy-start | bytes 148
  9.8 0.7 %copy-start.3 = (f32[12]{0:T(128)S(1)}, f32[12]{0:T(128)}, u32[]{:S(2)}) copy-start(f32[12]{0:T(128)} %param.13) | copy-start | bytes 148
  9.8 0.7 %copy-start.4 = (f32[24]{0:T(128)S(1)}, f32[24]{0:T(128)}, u32[]{:S(2)}) copy-start(f32[24]{0:T(128)} %param.15) | copy-start | bytes 292

commit v6 on v5

--- a/solution.py
+++ b/solution.py
@@ -90,7 +90,7 @@
             for piece in range(z.pieces):
                 at = first // 4 + piece
                 value = pieces[at] if 0 <= at < len(pieces) else empty
-                packed_ref[(to * slices + s) * z.pieces + piece] = value
+                packed_ref[to * slices + s, :, piece * z.half : (piece + 1) * z.half] = value
 
         for core in range(2):
             for member in range(members):
@@ -259,17 +259,15 @@
         return [side_by_side(pair) for pair in (evens, odds, odds_right, evens_left)]
 
     def lines_of(k, core):
-        pieces = []
-        for piece in range(z.pieces):
-            at = k * z.pieces + piece
-            pieces.append(sum(got_ref[source, core, at].astype(F32) for source in sources))
-        return stacked(pieces + blanks)
+        window = sum(got_ref[source, core, k].astype(F32) for source in sources)
+        lines = [window[:, piece * n : (piece + 1) * n] for piece in range(z.pieces)]
+        return stacked(lines + blanks).astype(BF16)
 
     def leading(base):
         fields = []
         for k in range(0, group, 2):
             evens, odds = ([lines_of(base + k, core), lines_of(base + k + 1, core)] for core in range(2))
-            fields.append(stacked([stacked(blocks(evens, odds, lanes0)).astype(BF16), ones]))
+            fields.append(stacked(blocks(evens, odds, lanes0) + [ones]))
         firsts = [relu(nn_dot(k1_ref[...], field)) for field in fields]
         fields = []
         for first in firsts:
@@ -342,7 +340,7 @@
     )(volume)
     packed = pl.pallas_call(
         functools.partial(pack_kernel, z, chips, members),
-        out_shape=like((vols * members * slices * z.pieces, 4, z.half), BF16),
+        out_shape=like((vols * members * slices, 4, z.pieces * z.half), BF16),
         in_specs=[vmem] * 3,
         out_specs=vmem,
         compiler_params=pltpu.CompilerParams(vmem_limit_bytes=16 * 1024 * 1024),
@@ -353,7 +351,7 @@
         reduce_conv_weight, reduce_conv_bias, deep_weight, deep_offset,
     ))
     got = lax.all_to_all(packed, ("vol", "zs"), split_axis=0, concat_axis=0, tiled=True)
-    got = got.reshape(chips, 2, z.depth * z.pieces, 4, z.half)
+    got = got.reshape(chips, 2, z.depth, 4, z.pieces * z.half)
     prepared = pl.pallas_call(
         functools.partial(prepare_kernel, z, members),
         out_shape=(

time: 19.2 us -> 19.2 us (level)
  no operation moved by 1% of the time
where the time goes in v6:
time: 19.2 us; the launch traced here: 18.9 us
  starting transfers between devices  7.64 us (40%)
  waiting for transfers between devices  5.62 us (29%)
  Pallas kernels  3.84 us (20%)
  local copies, waits for them, and re-layouts  1.68 us (9%)
    all_to_all x1, starting transfers between devices, shards(): lax.all_to_all(packed, ('vol', 'zs'), split_axis=0, concat_axis=0, tiled=...  7.19 us
    all_to_all x1, waiting for transfers between devices, shards(): lax.all_to_all(packed, ('vol', 'zs'), split_axis=0, concat_axis=0, tiled=...  5.42 us
    pallas_call x1, Pallas kernels, shards(): pl.pallas_call(functools.partial(main_kernel, z, chips), out_shape=like((...  1.82 us
    unnamed x18, local copies, waits for them, and re-layouts  1.41 us
    pallas_call x1, Pallas kernels, shards(): pl.pallas_call(functools.partial(prepare_kernel, z, members), out_shape=(...  1.1 us
    pallas_call x1, Pallas kernels, shards(): pl.pallas_call(functools.partial(pack_kernel, z, chips, members), out_sha...  0.79 us
    ppermute x1, starting transfers between devices, shards(): other = lax.ppermute(volume, 'vol', [(v, v ^ 1) for v in range(vols)])  0.45 us
  transfers between devices with their start and end apart: 2, of which 2 were waited for; matrix products, arithmetic and copies ran while one was open for 1% of the time, Pallas kernels for 7%

profile of v6, /device:TPU:0, one launch (start us, length us, event | category | flops | bytes accessed | tf_op | source)
XLA Modules:
  0.0 18.9 jit_solution(12574059822435642527)
XLA Ops:
  0.0 0.5 %collective-permute-start = (bf16[1,32,256]{2,1,0:T(8,128)(2,1)}, bf16[1,32,256]{2,1,0:T(8,128)(2,1)S(1)}, u32[]{:S(2)}, u32[]{:S(2)}) collective-permute-start(bf16[1,32,256]{2,1,0:T(8,128)(2,1)} %own_ref.1), channel_id=1, source_target_pairs={{0,8},{8,0},{16,24},{24,16},{1,9},{9,1},{17,25},{25,17},{2,10},{10... | collective-permute-start | bytes 49160 | tf_op jit(solution)/shard_map/ppermute | solution.py:331
  0.5 0.0 copy-start.6
  0.5 0.7 %copy-done.6 = bf16[1,32,256]{2,1,0:T(8,128)(2,1)S(1)} copy-done((bf16[1,32,256]{2,1,0:T(8,128)(2,1)S(1)}, bf16[1,32,256]{2,1,0:T(8,128)(2,1)}, u32[]{:S(2)}) %copy-start.6) | copy-done | bytes 16408
  1.2 0.1 sort.1
  1.3 0.2 %collective-permute-done.other_ref = bf16[1,32,256]{2,1,0:T(8,128)(2,1)S(1)} collective-permute-done((bf16[1,32,256]{2,1,0:T(8,128)(2,1)}, bf16[1,32,256]{2,1,0:T(8,128)(2,1)S(1)}, u32[]{:S(2)}, u32[]{:S(2)}) %collective-permute-start) | collective-permute-done | bytes 16416 | tf_op jit(solution)/shard_map/ppermute | solution.py:331
  1.5 0.8 %pack.1 = bf16[32,4,384]{2,1,0:T(4,128)(2,1)} custom-call(f32[1,32,128]{2,1,0:T(8,128)S(1)} %get-tuple-element.20.own_ref, bf16[256,128]{1,0:T(8,128)(2,1)S(1)} %get-tuple-element.21.sort_ref, bf16[1,32,256]{2,1,0:T(8,128)(2,1)S(1)} %collective-permute-done.other_ref), custom_call_target="tpu_custom_call" | custom-call | tf_op jit(solution)/shard_map/pack/pallas_call | solution.py:341
  2.3 0.0 copy-start.8
  2.3 0.0 copy-start.7
  2.3 7.2 %all-to-all-start = ((bf16[32,4,384]{2,1,0:T(4,128)(2,1)}), bf16[32,4,384]{2,1,0:T(4,128)(2,1)S(1)}, u32[]{:S(2)}, u32[]{:S(2)}) async-start(bf16[32,4,384]{2,1,0:T(4,128)(2,1)} %pack.1), calls=%async_computation | async-start | bytes 196608 | tf_op jit(solution)/shard_map/all_to_all | solution.py:353
  9.5 0.0 copy-done.8
  9.5 0.0 copy-done.7
  9.5 0.0 copy-start
  9.5 0.0 copy-start.5
  9.6 0.3 %copy.11.w4_ref = bf16[27,24,24]{2,1,0:T(8,128)(2,1)S(1)} copy(bf16[27,24,24]{0,2,1:T(8,128)(2,1)S(1)} %copy-done.7) | data formatting | bytes 62208 | tf_op jit(solution)/shard_map/optimization_barrier | solution.py:349
  9.8 0.0 copy-start.1
  9.8 0.0 copy-start.2
  9.8 0.0 copy-start.3
  9.8 0.0 copy-start.4
  9.9 0.4 %copy-done = bf16[9,12,12]{2,1,0:T(8,128)(2,1)S(1)} copy-done((bf16[9,12,12]{2,1,0:T(8,128)(2,1)S(1)}, bf16[9,12,12]{2,1,0:T(8,128)(2,1)}, u32[]{:S(2)}) %copy-start) | copy-done | bytes 2616
  10.3 0.0 copy-done.5
  10.3 0.2 %copy-done.1 = bf16[9,12]{1,0:T(8,128)(2,1)S(1)} copy-done((bf16[9,12]{1,0:T(8,128)(2,1)S(1)}, bf16[9,12]{1,0:T(8,128)(2,1)}, u32[]{:S(2)}) %copy-start.1) | copy-done | bytes 240
  10.5 0.0 copy-done.2
  10.5 0.0 copy-done.3
  10.5 0.0 copy-done.4
  10.5 1.1 %prepare.1 = (bf16[256,80]{1,0:T(8,128)(2,1)S(1)}, bf16[192,512]{1,0:T(8,128)(2,1)S(1)}, bf16[96,208]{1,0:T(8,128)(2,1)S(1)}, bf16[144,304]{1,0:T(8,128)(2,1)S(1)}) custom-call(bf16[9,12]{1,0:T(8,128)(2,1)S(1)} %copy-done.1, f32[1,12]{1,0:T(1,128)S(1)} %bitcast.7, bf16[9,12,12]{2,1,0:T(8,128)(2,1)S(1)} %copy-done, f32[1,12]{1,0:T(1,128)S(1)} %bitcast.8, ...), custom_call_target="tpu_custom_call" | custom-call | flops 50000000 | bytes 1000000 | tf_op jit(solution)/shard_map/prepare/pallas_call | solution.py:355
  11.6 5.4 %all-to-all-done = bf16[32,4,384]{2,1,0:T(4,128)(2,1)S(1)} async-done(((bf16[32,4,384]{2,1,0:T(4,128)(2,1)}), bf16[32,4,384]{2,1,0:T(4,128)(2,1)S(1)}, u32[]{:S(2)}, u32[]{:S(2)}) %all-to-all-start) | async-done | bytes 98336 | tf_op jit(solution)/shard_map/all_to_all | solution.py:353
  17.1 1.8 %encode.1 = bf16[8,48,128]{2,1,0:T(8,128)(2,1)} custom-call(bf16[2,2,8,4,384]{4,3,2,1,0:T(4,128)(2,1)S(1)} %bitcast.6, bf16[256,80]{1,0:T(8,128)(2,1)S(1)} %get-tuple-element.31.k1_ref, bf16[192,512]{1,0:T(8,128)(2,1)S(1)} %get-tuple-element.32.k2_ref, bf16[96,208]{1,0:T(8,128)(2,1)S(1)} %get-tuple-element.33.k3_ref, ...), custom_call_target="tpu_custom_call" | custom-call | flops 2000000000 | bytes 2000000 | tf_op jit(solution)/shard_map/encode/pallas_call | solution.py:371
  (1 shorter events, 0.0 us)
Async XLA Ops:
  0.0 1.5 %collective-permute-start = (bf16[1,32,256]{2,1,0:T(8,128)(2,1)}, bf16[1,32,256]{2,1,0:T(8,128)(2,1)S(1)}, u32[]{:S(2)}, u32[]{:S(2)}) collective-permute-start(bf16[1,32,256]{2,1,0:T(8,128)(2,1)} %own_ref.1), channel_id=1, source_target_pairs={{0,8},{8,0},{16,24},{24,16},{1,9},{9,1},{17,25},{25,17},{2,10},{10... | collective-permute-start | bytes 49160 | tf_op jit(solution)/shard_map/ppermute | solution.py:331
  0.5 0.7 %copy-start.6 = (bf16[1,32,256]{2,1,0:T(8,128)(2,1)S(1)}, bf16[1,32,256]{2,1,0:T(8,128)(2,1)}, u32[]{:S(2)}) copy-start(bf16[1,32,256]{2,1,0:T(8,128)(2,1)} %own_ref.1) | copy-start | bytes 49156
  2.3 7.2 %copy-start.8 = (bf16[4,12,24]{2,0,1:T(4,128)(2,1)S(1)}, bf16[4,12,24]{2,0,1:T(4,128)(2,1)}, u32[]{:S(2)}) copy-start(bf16[4,12,24]{2,0,1:T(4,128)(2,1)} %param.14) | copy-start | bytes 6916
  2.3 7.2 %copy-start.7 = (bf16[27,24,24]{0,2,1:T(8,128)(2,1)S(1)}, bf16[27,24,24]{0,2,1:T(8,128)(2,1)}, u32[]{:S(2)}) copy-start(bf16[27,24,24]{0,2,1:T(8,128)(2,1)} %param.16) | copy-start | bytes 93316
  2.3 14.8 %all-to-all-start = ((bf16[32,4,384]{2,1,0:T(4,128)(2,1)}), bf16[32,4,384]{2,1,0:T(4,128)(2,1)S(1)}, u32[]{:S(2)}, u32[]{:S(2)}) async-start(bf16[32,4,384]{2,1,0:T(4,128)(2,1)} %pack.1), calls=%async_computation | async-start | bytes 196608 | tf_op jit(solution)/shard_map/all_to_all | solution.py:353
  9.5 0.8 %copy-start = (bf16[9,12,12]{2,1,0:T(8,128)(2,1)S(1)}, bf16[9,12,12]{2,1,0:T(8,128)(2,1)}, u32[]{:S(2)}) copy-start(bf16[9,12,12]{2,1,0:T(8,128)(2,1)} %w2_ref) | copy-start | bytes 7780
  9.5 0.8 %copy-start.5 = (f32[24]{0:T(128)S(1)}, f32[24]{0:T(128)}, u32[]{:S(2)}) copy-start(f32[24]{0:T(128)} %param.17) | copy-start | bytes 292
  9.8 0.7 %copy-start.1 = (bf16[9,12]{1,0:T(8,128)(2,1)S(1)}, bf16[9,12]{1,0:T(8,128)(2,1)}, u32[]{:S(2)}) copy-start(bf16[9,12]{1,0:T(8,128)(2,1)} %w1_ref) | copy-start | bytes 652
  9.8 0.7 %copy-start.2 = (f32[12]{0:T(128)S(1)}, f32[12]{0:T(128)}, u32[]{:S(2)}) copy-start(f32[12]{0:T(128)} %param.11) | copy-start | bytes 148
  9.8 0.7 %copy-start.3 = (f32[12]{0:T(128)S(1)}, f32[12]{0:T(128)}, u32[]{:S(2)}) copy-start(f32[12]{0:T(128)} %param.13) | copy-start | bytes 148
  9.8 0.7 %copy-start.4 = (f32[24]{0:T(128)S(1)}, f32[24]{0:T(128)}, u32[]{:S(2)}) copy-start(f32[24]{0:T(128)} %param.15) | copy-start | bytes 292
